TPU v7x, 256 devices: a whole 4x4x8 slice. The times are simulated.
256 devices in a mesh: dp: 16 (over z, x_lo), pencil: 16 (over x_hi, y, core).
Axes of the slice: x: 4 (x_hi: 2, x_lo: 2; x = x_hi * 2 + x_lo), y: 4, z: 8, core: 2. Of those that a mesh axis runs over, the one named last changes fastest.
Arguments:
- clips: bfloat16 [32, 64, 512, 512], P('dp', None, 'pencil'), may hold values from -6 to 6
- cotangent: bfloat16 [32, 64, 512, 512], P('dp', None, 'pencil'), may hold values from -6 to 6
- spectral_weight: bfloat16 [64, 64, 64, 128], P(None, 'pencil'), may hold values from -3 to 3
- point_weight: bfloat16 [64, 64], replicated, may hold values from -0.75 to 0.75
- bias: bfloat16 [64], replicated, may hold values from -3 to 3
Outputs:
- input_grad: bfloat16 [32, 64, 512, 512], P('dp', None, 'pencil')
- spectral_grad: float32 [64, 64, 64, 128], P('dp', 'pencil')
All inputs are finite; a program needn't handle non-finite values.
Results may differ from a plain program's by a relative error of at most 0.029.
Values may be sent and summed in bfloat16 or wider, within the bound.
A program may use at most 192 MiB of HBM per device.

v0:
```python
import functools
import math

import jax
import jax.numpy as jnp
import ml_dtypes
import numpy as np
from jax import lax
from jax.experimental import pallas as pl
from jax.experimental.pallas import tpu as pltpu
from jax.sharding import PartitionSpec as P

TWO_PI = 2.0 * math.pi
MESH = pl.DeviceIdType.MESH
BF = jnp.bfloat16
F32 = jnp.float32
GROUP = 8
HALVES = 2
TN = (((0,), (0,)), ((), ()))
NT = (((1,), (1,)), ((), ()))
NN = (((1,), (0,)), ((), ()))


def dot(a, b, dims=NN):
    return lax.dot_general(a, b, dims, preferred_element_type=F32)


def tables():
    w = np.arange(512)
    g, half, j4 = np.meshgrid(np.arange(8), np.arange(2), np.arange(4), indexing="ij")
    j = ((half * 8 + g) * 4 + j4).reshape(8, 8)
    phase = (j[:, :, None] * w % 512) * (TWO_PI / 512)
    col = np.stack([np.cos(phase), np.sin(phase)], axis=1).reshape(128, 512)
    k = np.arange(64)
    f = np.where(k < 32, k, 448 + k)
    h = np.arange(512)
    phase = (h[:, None] * f[None, :] % 512) * (TWO_PI / 512)
    ca, sa = np.cos(phase), np.sin(phase)
    r = np.stack([ca, sa], axis=1).reshape(2, 8, 32, 128)
    eye = np.eye(4)
    fwd = np.einsum("xshn,cd->xschdn", r, eye).reshape(2, 1024, 512)
    first = np.stack([ca, -sa], axis=1)
    second = np.stack([-sa, -ca], axis=1)
    inv = np.stack([first, second], axis=1).reshape(2, 8, 32, 2, 128)
    inv = np.einsum("xshqn,cd->xcnsqdh", inv, eye).reshape(2, 512, 2048)
    perm = np.einsum("ad,be,cf->abcfed", np.eye(4), np.eye(16), np.eye(8)).reshape(512, 512)
    return [np.asarray(t, np.float32).astype(ml_dtypes.bfloat16) for t in (col, fwd, inv, perm)]


def derivative(z):
    a = jnp.abs(z)
    e = jnp.exp(z * z * -0.5)
    t = 1.0 / (1.0 + (0.3275911 / math.sqrt(2.0)) * a)
    poly = 1.061405429 * 0.5
    for c in (-1.453152027, 1.421413741, -0.284496736, 0.254829592):
        poly = poly * t + 0.5 * c
    q = e * (poly * t - a * (1.0 / math.sqrt(TWO_PI)))
    return jnp.where(z >= 0.0, 1.0 - q, q)


def kernel(
    dps,
    clips, cot, weight, pw, bias, col_h, fwd_h, inv_h, perm_h,
    out, sgrad,
    xv, cv, wv, col, fwd, inv, perm,
    send, recv, zs, dz, xp, xr, ya,
    xbf, xb, xbr, gbf, gb, gbr, dd, y3, kf, kb, bcol,
    in_sem, a2a_send, a2a_recv, x_send, x_recv, dp_send, dp_recv, out_sem,
):
    pen = lax.axis_index("pencil")
    dpi = lax.axis_index("dp")
    half = pen // GROUP
    me = pen % GROUP
    other = 1 - half
    partner = other * GROUP + me

    loads = [
        pltpu.make_async_copy(clips.at[0], xv.at[0], in_sem.at[0]),
        pltpu.make_async_copy(col_h, col, in_sem.at[1]),
        pltpu.make_async_copy(clips.at[1], xv.at[1], in_sem.at[2]),
        pltpu.make_async_copy(fwd_h.at[half], fwd, in_sem.at[3]),
        pltpu.make_async_copy(perm_h, perm, in_sem.at[4]),
        pltpu.make_async_copy(weight, wv, in_sem.at[5]),
        pltpu.make_async_copy(inv_h.at[half], inv, in_sem.at[6]),
        pltpu.make_async_copy(cot, cv, in_sem.at[7]),
    ]
    for copy in loads:
        copy.start()

    barrier = pltpu.get_barrier_semaphore()

    def greet_group(r, carry):
        peer = half * GROUP + (me + r) % GROUP
        pl.semaphore_signal(barrier, inc=1, device_id={"pencil": peer}, device_id_type=MESH)
        return carry

    lax.fori_loop(1, GROUP, greet_group, 0)
    pl.semaphore_signal(barrier, inc=1, device_id={"pencil": partner}, device_id_type=MESH)

    def greet_dp(r, carry):
        pl.semaphore_signal(barrier, inc=1, device_id={"dp": (dpi + r) % dps}, device_id_type=MESH)
        return carry

    if dps > 1:
        lax.fori_loop(1, dps, greet_dp, 0)

    lane = lax.broadcasted_iota(jnp.int32, (1, 128), 1)
    low = lane < 64
    sign = jnp.where(low, 1.0, -1.0).astype(F32)

    def columns(values, b, phase):
        def step(n, carry):
            rows = values[b, pl.ds(pl.multiple_of(n * 8, 8), 8)].reshape(256, 512)
            part = dot(col[...], rows, NT)
            for i in range(2):
                piece = part[:, i * 128 : (i + 1) * 128].reshape(8, 16, 128).astype(BF)
                at = pl.multiple_of((2 * n + i) * 16, 16)
                send[phase, b, :, pl.ds(at, 16), :] = piece
            return carry

        lax.fori_loop(0, 8, step, 0)

    def scatter(b, phase):
        def step(r, carry):
            to = (me + r) % GROUP
            pltpu.make_async_remote_copy(
                src_ref=send.at[phase, b, to],
                dst_ref=recv.at[phase, b, me],
                send_sem=a2a_send.at[phase, b],
                recv_sem=a2a_recv.at[phase, b],
                device_id={"pencil": half * GROUP + to},
                device_id_type=MESH,
            ).start()
            return carry

        lax.fori_loop(1, GROUP, step, 0)
        pltpu.make_async_copy(
            send.at[phase, b, me], recv.at[phase, b, me], a2a_recv.at[phase, b]
        ).start()

    def arrived(b, phase):
        whole = recv.at[phase, b]
        pltpu.make_async_copy(whole, whole, a2a_recv.at[phase, b]).wait()

    def rows_forward(b, phase, which):
        arrived(b, phase)
        lhs = jnp.concatenate([recv[phase, b, s] for s in range(GROUP)], axis=1)
        pieces = []
        for c4 in range(4):
            part = dot(lhs, fwd[:, c4 * 128 : (c4 + 1) * 128]).reshape(16, 2, 8, 128)
            cosine = part[:, 0].reshape(128, 128)
            sine = part[:, 1].reshape(128, 128)
            pieces.append((cosine * sign - pltpu.roll(sine, 64, 1)).astype(BF))
        spec = dot(jnp.concatenate(pieces, axis=0), perm[...], TN).astype(BF)
        xp[which, b, 0] = spec[:, :256]
        xp[which, b, 1] = spec[:, 256:]
        pltpu.make_async_remote_copy(
            src_ref=xp.at[which, b, other],
            dst_ref=xr.at[which, b],
            send_sem=x_send.at[which, b],
            recv_sem=x_recv.at[which, b],
            device_id={"pencil": partner},
            device_id_type=MESH,
        ).start()

    def x_wait(which, b, ref):
        pltpu.make_async_copy(ref, ref, x_recv.at[which, b]).wait()

    def spectrum(which, b):
        x_wait(which, b, xr.at[which, b])
        return xp[which, b, half].astype(F32) + xr[which, b].astype(F32)

    def to_owner(src, dst, i):
        def step(r, carry):
            to = (dpi + r) % dps
            pltpu.make_async_remote_copy(
                src_ref=src.at[to],
                dst_ref=dst.at[dpi],
                send_sem=dp_send.at[i],
                recv_sem=dp_recv.at[i],
                device_id={"dp": to},
                device_id_type=MESH,
            ).start()
            return carry

        if dps > 1:
            lax.fori_loop(1, dps, step, 0)
        pltpu.make_async_copy(src.at[dpi], dst.at[dpi], dp_recv.at[i]).start()

    def give_partner(i, b):
        pltpu.make_async_remote_copy(
            src_ref=ya.at[i, b, half],
            dst_ref=ya.at[i, b, half],
            send_sem=x_send.at[2 + i, b],
            recv_sem=x_recv.at[2 + i, b],
            device_id={"pencil": partner},
            device_id_type=MESH,
        ).start()

    def rows_back(i, b, phase):
        x_wait(2 + i, b, ya.at[i, b, other])
        turned = dot(perm[:, :256], ya[i, b, 0], NT) + dot(perm[:, 256:], ya[i, b, 1], NT)
        turned = turned.astype(BF)
        lhs = jnp.concatenate([turned[c * 128 : (c + 1) * 128] for c in range(4)], axis=1)
        for s in range(GROUP):
            lines = dot(lhs, inv[:, s * 256 : (s + 1) * 256])
            both = jnp.concatenate(
                [lines[:, :128].reshape(16, 8, 128), lines[:, 128:].reshape(16, 8, 128)], axis=1
            )
            send[phase, b, s] = both.reshape(256, 128).astype(BF)
        scatter(b, phase)

    def field(b, phase, n):
        at = pl.multiple_of(n * 16, 16)
        lines = recv[phase, b, :, pl.ds(at, 16), :].reshape(128, 128)
        return dot(lines, col[...], TN)

    def mix_points(values, b, matrix, add):
        def step(t, carry):
            at = pl.multiple_of(t * 16, 16)
            for n in range(2):
                lanes = slice(n * 256, (n + 1) * 256)
                tile = values[b, :, pl.ds(at, 16), lanes].astype(F32)
                for i in range(2):
                    rows = tile[:, i * 8 : (i + 1) * 8].reshape(512, 256).astype(BF)
                    got = dot(matrix[...], rows)
                    if add is not None:
                        got = got + jnp.concatenate([add[...]] * 2, axis=1)
                    to = pl.multiple_of(t * 16 + i * 8, 8)
                    zs[b, :, pl.ds(to, 8), lanes] = got.reshape(64, 8, 256)
            return carry

        lax.fori_loop(0, 2, step, 0)

    loads[0].wait()
    loads[1].wait()
    columns(xv, 0, 0)
    pl.semaphore_wait(barrier, GROUP - 1 + 1 + dps - 1)
    scatter(0, 0)
    loads[2].wait()
    columns(xv, 1, 0)
    scatter(1, 0)

    row = lax.broadcasted_iota(jnp.int32, (512, 64), 0)
    lanes64 = lax.broadcasted_iota(jnp.int32, (512, 64), 1)
    spread = jnp.where(row // 8 == lanes64, 1.0, 0.0).astype(BF)
    same = (
        lax.broadcasted_iota(jnp.int32, (512, 512), 0) % 8
        == lax.broadcasted_iota(jnp.int32, (512, 512), 1) % 8
    )
    kf[...] = jnp.where(same, dot(dot(spread, pw[...], NT).astype(BF), spread, NT), 0.0).astype(BF)
    kb[...] = jnp.where(same, dot(dot(spread, pw[...]).astype(BF), spread, NT), 0.0).astype(BF)
    biased = (spread.astype(F32) * bias[...].astype(F32)).astype(BF)
    bcol[...] = dot(biased, jnp.ones((64, 128), BF))
    mix_points(xv, 0, kf, bcol)
    mix_points(xv, 1, kf, bcol)

    loads[3].wait()
    loads[4].wait()
    rows_forward(0, 0, 0)
    rows_forward(1, 0, 0)

    for b in range(2):
        spec = spectrum(0, b)
        for ri in range(2):
            for j in range(4):
                for p in range(2):
                    if p == j // 2:
                        part = spec[ri * 64 : (ri + 1) * 64, p * 128 : (p + 1) * 128]
                        part = jnp.where(low if j % 2 == 0 else jnp.logical_not(low), part, 0.0)
                    else:
                        part = jnp.zeros((64, 128), F32)
                    xbf[p, pl.ds(ri * 8 + j * 2 + b, 64, stride=16), :] = part
    per = 1024 // dps
    for d in range(dps):
        for p in range(2):
            xb[d, :, p * 128 : (p + 1) * 128] = xbf[p, d * per : (d + 1) * per, :].astype(BF)
    to_owner(xb, xbr, 0)

    loads[5].wait()
    row8 = lax.broadcasted_iota(jnp.int32, (8, 128), 0)
    zero_mode = jnp.logical_and(row8 < 2, pen == 0)
    scale8 = jnp.where(zero_mode, 1.0, 2.0).astype(F32) / 262144.0
    kper = 64 // dps

    def mix_step(d, carry):
        for i in range(kper):
            k = d * kper + i
            got = dot(xb[d, i * 16 : (i + 1) * 16, :], wv[k].reshape(256, 128))
            y = got[:8] - sign * pltpu.roll(got[8:], 64, 1)
            y3[pl.ds(pl.multiple_of(k * 8, 8), 8), :] = y * scale8
        return carry

    lax.fori_loop(0, dps, mix_step, 0)
    for b in range(2):
        for p in range(2):
            first = y3[pl.ds(4 * p + b, 64, stride=8), :]
            second = y3[pl.ds(4 * p + 2 + b, 64, stride=8), :]
            real = jnp.where(low, first, pltpu.roll(second, 64, 1))
            imag = jnp.where(low, pltpu.roll(first, 64, 1), second)
            ya[0, b, half, 0:64, p * 128 : (p + 1) * 128] = real.astype(BF)
            ya[0, b, half, 64:128, p * 128 : (p + 1) * 128] = imag.astype(BF)
        give_partner(0, b)
    loads[6].wait()
    rows_back(0, 0, 1)
    rows_back(0, 1, 1)

    loads[7].wait()
    for b in range(2):
        arrived(b, 1)

        def act_step(n, carry, b=b):
            at = pl.ds(pl.multiple_of(n * 4, 4), 4)
            z = field(b, 1, n) + zs[b, at].reshape(128, 512)
            grad = cv[b, at].reshape(128, 512).astype(F32) * derivative(z)
            dz[b, at] = grad.astype(BF).reshape(4, 32, 512)
            return carry

        lax.fori_loop(0, 16, act_step, 0)
        columns(dz, b, 2)
        scatter(b, 2)
    mix_points(dz, 0, kb, None)
    mix_points(dz, 1, kb, None)

    rows_forward(0, 2, 1)
    rows_forward(1, 2, 1)
    scale_lane = jnp.where(jnp.logical_and(low, pen == 0), 1.0, 2.0).astype(F32) / 262144.0
    for b in range(2):
        spec = spectrum(1, b)
        for p in range(2):
            part = spec[:, p * 128 : (p + 1) * 128]
            part = part * (scale_lane if p == 0 else 2.0 / 262144.0)
            real, imag = part[:64], part[64:]
            real_r, imag_r = pltpu.roll(real, 64, 1), pltpu.roll(imag, 64, 1)
            for i, (re, im) in enumerate(
                ((jnp.where(low, real, imag_r), jnp.where(low, imag, real_r)),
                 (jnp.where(low, real_r, imag), jnp.where(low, imag_r, real)))
            ):
                row_at = (2 * p + i) * 2 + b
                gbf[pl.ds(row_at, 64, stride=16), :] = re
                gbf[pl.ds(8 + row_at, 64, stride=16), :] = im * sign
    for d in range(dps):
        gb[d] = gbf[d * per : (d + 1) * per, :].astype(BF)
    to_owner(gb, gbr, 1)

    def back_step(d, carry):
        for i in range(kper):
            k = d * kper + i
            got = dot(gb[d, i * 16 : (i + 1) * 16, :], wv[k].reshape(256, 128), NT)
            at = pl.ds(pl.multiple_of(k * 16, 16), 16)
            dd[0, at, :] = got[:, :128]
            dd[1, at, :] = got[:, 128:]
        return carry

    lax.fori_loop(0, dps, back_step, 0)
    for b in range(2):
        for p in range(2):
            for ri in range(2):
                first = dd[p, pl.ds(ri * 8 + 4 * p + b, 64, stride=16), :]
                second = dd[p, pl.ds(ri * 8 + 4 * p + 2 + b, 64, stride=16), :]
                ya[1, b, half, ri * 64 : (ri + 1) * 64, p * 128 : (p + 1) * 128] = jnp.where(
                    low, first, second
                ).astype(BF)
        give_partner(1, b)
    rows_back(1, 0, 3)
    rows_back(1, 1, 3)

    for i, ref in enumerate((xbr, gbr)):
        pltpu.make_async_copy(ref, ref, dp_recv.at[i]).wait()
    for k in range(kper):
        left = xbr[:, k * 16 : (k + 1) * 16, :].reshape(dps * 16, 256)
        right = gbr[:, k * 16 : (k + 1) * 16, :].reshape(dps * 16, 128)
        sgrad[k] = dot(left, right, TN).reshape(4, 64, 128)

    for b in range(2):
        arrived(b, 3)

        def out_step(n, carry, b=b):
            at = pl.ds(pl.multiple_of(n * 4, 4), 4)
            got = field(b, 3, n) + zs[b, at].reshape(128, 512)
            xv[b, at] = got.astype(BF).reshape(4, 32, 512)
            return carry

        lax.fori_loop(0, 16, out_step, 0)
        pltpu.make_async_copy(xv.at[b], out.at[b], out_sem.at[b]).start()

    for phase in range(4):
        for b in range(2):
            sent = send.at[phase, b, pl.ds(0, GROUP - 1)]
            pltpu.make_async_copy(sent, sent, a2a_send.at[phase, b]).wait()
            ref = xr.at[0, b]
            pltpu.make_async_copy(ref, ref, x_send.at[phase, b]).wait()
    if dps > 1:
        for i, ref in enumerate((xb, gb)):
            sent = ref.at[pl.ds(0, dps - 1)]
            pltpu.make_async_copy(sent, sent, dp_send.at[i]).wait()
    for b in range(2):
        pltpu.make_async_copy(xv.at[b], out.at[b], out_sem.at[b]).wait()


def shards(dps, clips, cotangent, spectral_weight, point_weight, bias):
    col, fwd, inv, perm = [jnp.asarray(t) for t in tables()]
    any_spec = pl.BlockSpec(memory_space=pl.ANY)
    vmem = pl.BlockSpec(memory_space=pltpu.VMEM)
    per = 1024 // dps
    dma = pltpu.SemaphoreType.DMA
    return pl.pallas_call(
        functools.partial(kernel, dps),
        out_shape=(
            jax.ShapeDtypeStruct((2, 64, 32, 512), BF),
            jax.ShapeDtypeStruct((64 // dps, 4, 64, 128), F32),
        ),
        in_specs=[any_spec] * 3 + [vmem] * 2 + [any_spec] * 4,
        out_specs=(any_spec, vmem),
        scratch_shapes=[
            pltpu.VMEM((2, 64, 32, 512), BF),
            pltpu.VMEM((2, 64, 32, 512), BF),
            pltpu.VMEM((64, 4, 64, 128), BF),
            pltpu.VMEM((128, 512), BF),
            pltpu.VMEM((1024, 512), BF),
            pltpu.VMEM((512, 2048), BF),
            pltpu.VMEM((512, 512), BF),
            pltpu.VMEM((4, 2, GROUP, 256, 128), BF),
            pltpu.VMEM((4, 2, GROUP, 256, 128), BF),
            pltpu.VMEM((2, 64, 32, 512), F32),
            pltpu.VMEM((2, 64, 32, 512), BF),
            pltpu.VMEM((2, 2, 2, 128, 256), BF),
            pltpu.VMEM((2, 2, 128, 256), BF),
            pltpu.VMEM((2, 2, 2, 128, 256), BF),
            pltpu.VMEM((2, 1024, 128), F32),
            pltpu.VMEM((dps, per, 256), BF),
            pltpu.VMEM((dps, per, 256), BF),
            pltpu.VMEM((1024, 128), F32),
            pltpu.VMEM((dps, per, 128), BF),
            pltpu.VMEM((dps, per, 128), BF),
            pltpu.VMEM((2, 1024, 128), F32),
            pltpu.VMEM((512, 128), F32),
            pltpu.VMEM((512, 512), BF),
            pltpu.VMEM((512, 512), BF),
            pltpu.VMEM((512, 128), F32),
            dma((8,)),
            dma((4, 2)),
            dma((4, 2)),
            dma((4, 2)),
            dma((4, 2)),
            dma((2,)),
            dma((2,)),
            dma((2,)),
        ],
        compiler_params=pltpu.CompilerParams(
            collective_id=0, has_side_effects=True, vmem_limit_bytes=60 * 1024 * 1024
        ),
        cost_estimate=pl.CostEstimate(
            flops=20_000_000_000, bytes_accessed=20_000_000, transcendentals=4_000_000
        ),
    )(clips, cotangent, spectral_weight, point_weight, bias.reshape(1, 64), col, fwd, inv, perm)


def solution(mesh):
    in_specs = (
        P("dp", None, "pencil", None),
        P("dp", None, "pencil", None),
        P(None, "pencil", None, None),
        P(),
        P(),
    )
    out_specs = (P("dp", None, "pencil", None), P("dp", "pencil", None, None))
    return jax.shard_map(
        functools.partial(shards, mesh.shape["dp"]),
        mesh=mesh,
        in_specs=in_specs,
        out_specs=out_specs,
        check_vma=False,
    )
```

profile of v0, /device:TPU:1, one launch (start us, length us, event | category | flops | bytes accessed | tf_op | source)
XLA Modules:
  0.0 113.2 jit_solution(2161391489525493790)
XLA Ops:
  0.6 107.0 %shard_map.104 = (bf16[2,64,32,512]{3,2,1,0:T(8,128)(2,1)}, f32[4,4,64,128]{3,2,1,0:T(8,128)}) custom-call(bf16[2,64,32,512]{3,2,1,0:T(8,128)(2,1)} %clips.1, bf16[2,64,32,512]{3,2,1,0:T(8,128)(2,1)} %cot.1, bf16[64,4,64,128]{3,2,1,0:T(8,128)(2,1)} %weight.1, bf16[64,64]{1,0:T(8,128)(2,1)} %pw.1, bf16[1,64]{1,0:T(2,128)(2,1)} %bitcast.1, ...), custom_call_target="tpu_custom_call" | custom-call | flops 20000000000 | bytes 20000000 | tf_op jit(solution)/shard_map/pallas_call | solution.py:407
  107.6 0.0 copy-start
  107.6 4.8 %copy.13 = bf16[2,64,32,512]{3,2,1,0:T(8,128)(2,1)} copy(bf16[2,64,32,512]{3,2,1,0:T(8,128)(2,1)} %get-tuple-element.4) | data formatting | bytes 8388608
  112.4 0.0 copy-done
  112.5 0.8 copy.14
Async XLA Ops:
  107.6 4.9 %copy-start = (f32[4,4,64,128]{3,2,1,0:T(8,128)S(1)}, f32[4,4,64,128]{3,2,1,0:T(8,128)}, u32[]{:S(2)}) copy-start(f32[4,4,64,128]{3,2,1,0:T(8,128)} %get-tuple-element.5) | copy-start | bytes 1572868
where the time goes:
time: 113 us
  Pallas kernels  107 us (95%)
  local copies, waits for them, and re-layouts  5.64 us (5%)
    pallas_call x1, Pallas kernels, shards(): pl.pallas_call(functools.partial(kernel, dps), out_shape=(jax.ShapeDtypeS...  107 us
    unnamed x4, local copies, waits for them, and re-layouts  5.64 us

commit v1 on v0

v1 whole, which is shorter than its diff:
```python
import functools
import math

import jax
import jax.numpy as jnp
import ml_dtypes
import numpy as np
from jax import lax
from jax.experimental import pallas as pl
from jax.experimental.pallas import tpu as pltpu
from jax.sharding import PartitionSpec as P

TWO_PI = 2.0 * math.pi
MESH = pl.DeviceIdType.MESH
BF = jnp.bfloat16
F32 = jnp.float32
GROUP = 8
TN = (((0,), (0,)), ((), ()))
NT = (((1,), (1,)), ((), ()))
NN = (((1,), (0,)), ((), ()))


def dot(a, b, dims=NN):
    return lax.dot_general(a, b, dims, preferred_element_type=F32)


def tables():
    w = np.arange(512)
    g, half, j4 = np.meshgrid(np.arange(8), np.arange(2), np.arange(4), indexing="ij")
    j = ((half * 8 + g) * 4 + j4).reshape(8, 8)
    phase = (j[:, :, None] * w % 512) * (TWO_PI / 512)
    col = np.stack([np.cos(phase), np.sin(phase)], axis=1).reshape(128, 512)
    k = np.arange(64)
    f = np.where(k < 32, k, 448 + k)
    h = np.arange(512)
    phase = (h[:, None] * f[None, :] % 512) * (TWO_PI / 512)
    ca, sa = np.cos(phase), np.sin(phase)
    r = np.stack([ca, sa], axis=1).reshape(2, 8, 32, 128)
    eye = np.eye(4)
    fwd = np.einsum("xshn,cd->xschdn", r, eye).reshape(2, 1024, 512)
    first = np.stack([ca, -sa], axis=1)
    second = np.stack([-sa, -ca], axis=1)
    inv = np.stack([first, second], axis=1).reshape(2, 8, 32, 2, 128)
    inv = np.einsum("xshqn,cd->xcnsqdh", inv, eye).reshape(2, 512, 2048)
    perm = np.einsum("ad,be,cf->abcfed", np.eye(4), np.eye(16), np.eye(8)).reshape(512, 512)
    return [np.asarray(t, np.float32).astype(ml_dtypes.bfloat16) for t in (col, fwd, inv, perm)]


def derivative(z):
    a = jnp.abs(z)
    e = jnp.exp(z * z * -0.5)
    d = 1.0 + (0.3275911 / math.sqrt(2.0)) * a
    t = pl.reciprocal(d, approx=True)
    t = t * (2.0 - d * t)
    poly = 1.061405429 * 0.5
    for c in (-1.453152027, 1.421413741, -0.284496736, 0.254829592):
        poly = poly * t + 0.5 * c
    q = e * (poly * t - a * (1.0 / math.sqrt(TWO_PI)))
    return jnp.where(z >= 0.0, 1.0 - q, q)


PEERS = ((2, 0), (2, 1), (1, 0), (3, 0), (1, 1), (3, 1), (0, 1))


def kernel(
    dps,
    clips, cot, weight, pw, bias, col_h, fwd_h, inv_h, perm_h,
    side, last, sgrad,
    xv, cv, wv, col, fwd, inv, perm,
    send, recv, zs, dz, xp, xr, ya,
    xbf, xb, xbr, gbf, gb, gbr, dd, y3, kf, kb, bcol,
    in_sem, clip_sem, a2a_send, a2a_recv, x_send, x_recv, dp_send, dp_recv, out_sem,
):
    pen = lax.axis_index("pencil")
    dpi = lax.axis_index("dp")
    half = pen // GROUP
    me = pen % GROUP
    other = 1 - half
    partner = other * GROUP + me
    per = 512 // dps
    kper = 64 // dps

    def clip_piece(b, n):
        at = pl.ds(n * 8, 8)
        return pltpu.make_async_copy(clips.at[b, at], xv.at[b, at], clip_sem.at[b, n])

    def load(src, dst, pieces, i):
        size = dst.shape[0] // pieces
        for n in range(pieces):
            at = pl.ds(n * size, size)
            pltpu.make_async_copy(src.at[at], dst.at[at], in_sem.at[i]).start()
        return pltpu.make_async_copy(dst, dst, in_sem.at[i]).wait

    col_wait = load(col_h, col, 1, 0)
    for b in range(2):
        for n in range(8):
            clip_piece(b, n).start()

    def peer_of(dy, dc):
        return (me // 2 + dy) % 4 * 2 + (me % 2 + dc) % 2

    barrier = pltpu.get_barrier_semaphore()
    for dy, dc in PEERS:
        peer = half * GROUP + peer_of(dy, dc)
        pl.semaphore_signal(barrier, inc=1, device_id={"pencil": peer}, device_id_type=MESH)
    pl.semaphore_signal(barrier, inc=1, device_id={"pencil": partner}, device_id_type=MESH)

    def greet_dp(r, carry):
        pl.semaphore_signal(barrier, inc=1, device_id={"dp": (dpi + r) % dps}, device_id_type=MESH)
        return carry

    if dps > 1:
        lax.fori_loop(1, dps, greet_dp, 0)

    lane = lax.broadcasted_iota(jnp.int32, (1, 128), 1)
    low = lane < 64
    sign = jnp.where(low, 1.0, -1.0).astype(F32)

    def slots(b, phase):
        return recv.at[phase, b] if phase < 3 else last.at[b]

    def columns(values, b, phase):
        def step(n, carry):
            if values is xv:
                clip_piece(b, n).wait()
            rows = values[b, pl.ds(pl.multiple_of(n * 8, 8), 8)].reshape(256, 512)
            part = dot(col[...], rows, NT)
            for i in range(2):
                piece = part[:, i * 128 : (i + 1) * 128].reshape(8, 16, 128).astype(BF)
                at = pl.multiple_of((2 * n + i) * 16, 16)
                send[phase, b, :, pl.ds(at, 16), :] = piece
            return carry

        lax.fori_loop(0, 8, step, 0, unroll=2)

    def send_one(b, phase, to):
        pltpu.make_async_remote_copy(
            src_ref=send.at[phase, b, to],
            dst_ref=slots(b, phase).at[me],
            send_sem=a2a_send.at[phase, b],
            recv_sem=a2a_recv.at[phase, b],
            device_id={"pencil": half * GROUP + to},
            device_id_type=MESH,
        ).start()

    def keep_own(b, phase):
        pltpu.make_async_copy(
            send.at[phase, b, me], slots(b, phase).at[me], a2a_recv.at[phase, b]
        ).start()

    def scatter(b, phase):
        for dy, dc in PEERS:
            send_one(b, phase, peer_of(dy, dc))
        keep_own(b, phase)

    def arrived(b, phase):
        whole = slots(b, phase)
        pltpu.make_async_copy(whole, whole, a2a_recv.at[phase, b]).wait()

    def rows_forward(b, phase, which):
        arrived(b, phase)
        lhs = jnp.concatenate([recv[phase, b, s] for s in range(GROUP)], axis=1)
        pieces = []
        for c4 in range(4):
            part = dot(lhs, fwd[:, c4 * 128 : (c4 + 1) * 128]).reshape(16, 2, 8, 128)
            cosine = part[:, 0].reshape(128, 128)
            sine = part[:, 1].reshape(128, 128)
            pieces.append((cosine * sign - pltpu.roll(sine, 64, 1)).astype(BF))
        spec = dot(jnp.concatenate(pieces, axis=0), perm[...], TN).astype(BF)
        xp[which, b, 0] = spec[:, :256]
        xp[which, b, 1] = spec[:, 256:]
        pltpu.make_async_remote_copy(
            src_ref=xp.at[which, b, other],
            dst_ref=xr.at[which, b],
            send_sem=x_send.at[which, b],
            recv_sem=x_recv.at[which, b],
            device_id={"pencil": partner},
            device_id_type=MESH,
        ).start()

    def x_wait(which, b, ref):
        pltpu.make_async_copy(ref, ref, x_recv.at[which, b]).wait()

    def spectrum(which, b):
        x_wait(which, b, xr.at[which, b])
        return xp[which, b, half].astype(F32) + xr[which, b].astype(F32)

    def to_owner(src, dst, i, b):
        def rows_of(d):
            return src.at[b, pl.ds(pl.multiple_of(d * per, per), per)]

        def step(r, carry):
            to = (dpi + r) % dps
            pltpu.make_async_remote_copy(
                src_ref=rows_of(to),
                dst_ref=dst.at[b, dpi],
                send_sem=dp_send.at[i, b],
                recv_sem=dp_recv.at[i, b],
                device_id={"dp": to},
                device_id_type=MESH,
            ).start()
            return carry

        if dps > 1:
            lax.fori_loop(1, dps, step, 0)
        pltpu.make_async_copy(rows_of(dpi), dst.at[b, dpi], dp_recv.at[i, b]).start()

    def give_partner(i, b):
        pltpu.make_async_remote_copy(
            src_ref=ya.at[i, b, half],
            dst_ref=ya.at[i, b, half],
            send_sem=x_send.at[2 + i, b],
            recv_sem=x_recv.at[2 + i, b],
            device_id={"pencil": partner},
            device_id_type=MESH,
        ).start()

    def rows_back(i, b, phase):
        x_wait(2 + i, b, ya.at[i, b, other])
        turned = dot(perm[:, :256], ya[i, b, 0], NT) + dot(perm[:, 256:], ya[i, b, 1], NT)
        turned = turned.astype(BF)
        lhs = jnp.concatenate([turned[c * 128 : (c + 1) * 128] for c in range(4)], axis=1)
        for dy, dc in PEERS + ((0, 0),):
            to = peer_of(dy, dc)
            lines = dot(lhs, inv[:, pl.ds(pl.multiple_of(to * 256, 256), 256)])
            both = jnp.concatenate(
                [lines[:, :128].reshape(16, 8, 128), lines[:, 128:].reshape(16, 8, 128)], axis=1
            )
            send[phase, b, to] = both.reshape(256, 128).astype(BF)
            if (dy, dc) == (0, 0):
                keep_own(b, phase)
            else:
                send_one(b, phase, to)

    def mix_points(values, b, matrix, add, tiles=(0, 2)):
        def step(t, carry):
            at = pl.multiple_of(t * 16, 16)
            for n in range(2):
                lanes = slice(n * 256, (n + 1) * 256)
                tile = values[b, :, pl.ds(at, 16), lanes].astype(F32)
                parts = []
                for i in range(2):
                    rows = tile[:, i * 8 : (i + 1) * 8].reshape(512, 256).astype(BF)
                    got = dot(matrix[...], rows)
                    if add is not None:
                        got = got + jnp.concatenate([add[...]] * 2, axis=1)
                        to = pl.multiple_of(t * 16 + i * 8, 8)
                        zs[b, :, pl.ds(to, 8), lanes] = got.reshape(64, 8, 256)
                    parts.append(got.reshape(64, 8, 256))
                if add is None:
                    xv[b, :, pl.ds(at, 16), lanes] = jnp.concatenate(parts, axis=1).astype(BF)
            return carry

        lax.fori_loop(*tiles, step, 0)

    row16 = lax.broadcasted_iota(jnp.int32, (16, 128), 0)
    scale = jnp.where(pen == 0, 1.0, 2.0).astype(F32) / 262144.0
    scale_lane = jnp.where(jnp.logical_and(low, pen == 0), 1.0, 2.0).astype(F32) / 262144.0

    def mix_modes(b):
        spec = spectrum(0, b)
        for ri in range(2):
            for j in range(4):
                for p in range(2):
                    if p == j // 2:
                        part = spec[ri * 64 : (ri + 1) * 64, p * 128 : (p + 1) * 128]
                        part = jnp.where(low if j % 2 == 0 else jnp.logical_not(low), part, 0.0)
                    else:
                        part = jnp.zeros((64, 128), F32)
                    xbf[p, pl.ds(ri * 4 + j, 64, stride=8), :] = part
        for p in range(2):
            xb[b, :, p * 128 : (p + 1) * 128] = xbf[p].astype(BF)
        to_owner(xb, xbr, 0, b)

        def step(n, carry):
            for i in range(8):
                pair = n * 8 + i
                at = pl.multiple_of(pair * 16, 16)
                both = jnp.concatenate(
                    [wv[2 * pair].reshape(256, 128), wv[2 * pair + 1].reshape(256, 128)], axis=1
                )
                got = dot(xb[b, pl.ds(at, 16), :], both)
                y3[pl.ds(at, 8), :] = got[:8, :128]
                y3[pl.ds(at + 8, 8), :] = got[8:, 128:]
            return carry

        lax.fori_loop(0, 4, step, 0)
        modes = []
        for j in range(4):
            real = y3[pl.ds(j, 64, stride=8), :]
            imag = y3[pl.ds(4 + j, 64, stride=8), :]
            mixed = real - sign * pltpu.roll(imag, 64, 1)
            modes.append(mixed * (scale if j == 0 else 2.0 / 262144.0))
        for p in range(2):
            first, second = modes[2 * p], modes[2 * p + 1]
            real = jnp.where(low, first, pltpu.roll(second, 64, 1))
            imag = jnp.where(low, pltpu.roll(first, 64, 1), second)
            ya[0, b, half, 0:64, p * 128 : (p + 1) * 128] = real.astype(BF)
            ya[0, b, half, 64:128, p * 128 : (p + 1) * 128] = imag.astype(BF)
        give_partner(0, b)

    def grad_modes(b):
        spec = spectrum(1, b)
        for p in range(2):
            part = spec[:, p * 128 : (p + 1) * 128]
            part = part * (scale_lane if p == 0 else 2.0 / 262144.0)
            real, imag = part[:64], part[64:]
            real_r, imag_r = pltpu.roll(real, 64, 1), pltpu.roll(imag, 64, 1)
            for i, (re, im) in enumerate(
                ((jnp.where(low, real, imag_r), jnp.where(low, imag, real_r)),
                 (jnp.where(low, real_r, imag), jnp.where(low, imag_r, real)))
            ):
                gbf[pl.ds(2 * p + i, 64, stride=8), :] = re
                gbf[pl.ds(4 + 2 * p + i, 64, stride=8), :] = im * sign
        gb[b] = gbf[...].astype(BF)
        to_owner(gb, gbr, 1, b)

        def step(n, carry):
            for i in range(8):
                pair = n * 8 + i
                at = pl.multiple_of(pair * 16, 16)
                got = dot(gb[b, pl.ds(at, 16), :], wv[pl.ds(2 * pair, 2)].reshape(512, 128), NT)
                for p in range(2):
                    dd[p, pl.ds(at, 8), :] = got[:8, p * 128 : (p + 1) * 128]
                    dd[p, pl.ds(at + 8, 8), :] = got[8:, 256 + p * 128 : 384 + p * 128]
            return carry

        lax.fori_loop(0, 4, step, 0)
        for p in range(2):
            for ri in range(2):
                first = dd[p, pl.ds(ri * 4 + 2 * p, 64, stride=8), :]
                second = dd[p, pl.ds(ri * 4 + 2 * p + 1, 64, stride=8), :]
                ya[1, b, half, ri * 64 : (ri + 1) * 64, p * 128 : (p + 1) * 128] = jnp.where(
                    low, first, second
                ).astype(BF)
        give_partner(1, b)

    def activation(b, chunks):
        def step(n, carry):
            at = pl.ds(pl.multiple_of(n * 4, 4), 4)
            lines = recv[1, b, :, pl.ds(pl.multiple_of(n * 16, 16), 16), :].reshape(128, 128)
            z = dot(lines, col[...], TN) + zs[b, at].reshape(128, 512)
            grad = cv[b, at].reshape(128, 512).astype(F32) * derivative(z)
            dz[b, at] = grad.astype(BF).reshape(4, 32, 512)
            return carry

        lax.fori_loop(*chunks, step, 0, unroll=4)

    def bypass(b):
        mix_points(dz, b, kb, None)
        pltpu.make_async_copy(xv.at[b], side.at[b], out_sem.at[b]).start()

    def weight_grad(b):
        for i, ref in enumerate((xbr, gbr)):
            pltpu.make_async_copy(ref.at[b], ref.at[b], dp_recv.at[i, b]).wait()
        first_rows = jnp.where(row16 < 8, 1.0, 0.0).astype(F32)
        for pair in range(kper // 2):
            at = slice(pair * 16, (pair + 1) * 16)
            left = xbr[b, :, at, :].reshape(dps * 16, 256)
            right = gbr[b, :, at, :].astype(F32)
            head = (right * first_rows).astype(BF).reshape(dps * 16, 128)
            tail = (right * (1.0 - first_rows)).astype(BF).reshape(dps * 16, 128)
            got = dot(left, jnp.concatenate([head, tail], axis=1), TN)
            for i in range(2):
                part = got[:, i * 128 : (i + 1) * 128].reshape(4, 64, 128)
                sgrad[2 * pair + i] = part if b == 0 else sgrad[2 * pair + i] + part

    col_wait()
    columns(xv, 0, 0)
    pl.semaphore_wait(barrier, GROUP - 1 + 1 + dps - 1)
    scatter(0, 0)
    fwd_wait = load(fwd_h.at[half], fwd, 4, 1)
    perm_wait = load(perm_h, perm, 2, 2)
    columns(xv, 1, 0)
    scatter(1, 0)
    weight_wait = load(weight, wv, 16, 3)
    inv_wait = load(inv_h.at[half], inv, 4, 4)
    cot_waits = [load(cot.at[b], cv.at[b], 8, 5 + b) for b in range(2)]

    row = lax.broadcasted_iota(jnp.int32, (512, 64), 0)
    lanes64 = lax.broadcasted_iota(jnp.int32, (512, 64), 1)
    spread = jnp.where(row // 8 == lanes64, 1.0, 0.0).astype(BF)
    same = (
        lax.broadcasted_iota(jnp.int32, (512, 512), 0) % 8
        == lax.broadcasted_iota(jnp.int32, (512, 512), 1) % 8
    )
    kf[...] = jnp.where(same, dot(dot(spread, pw[...], NT).astype(BF), spread, NT), 0.0).astype(BF)
    kb[...] = jnp.where(same, dot(dot(spread, pw[...]).astype(BF), spread, NT), 0.0).astype(BF)
    biased = (spread.astype(F32) * bias[...].astype(F32)).astype(BF)
    bcol[...] = dot(biased, jnp.ones((64, 128), BF))
    mix_points(xv, 0, kf, bcol)

    fwd_wait()
    perm_wait()
    rows_forward(0, 0, 0)
    mix_points(xv, 1, kf, bcol)
    rows_forward(1, 0, 0)
    weight_wait()
    mix_modes(0)
    mix_modes(1)
    inv_wait()
    rows_back(0, 0, 1)
    rows_back(0, 1, 1)

    arrived(0, 1)
    cot_waits[0]()
    activation(0, (0, 16))
    columns(dz, 0, 2)
    scatter(0, 2)
    arrived(1, 1)
    cot_waits[1]()
    activation(1, (0, 16))
    columns(dz, 1, 2)
    scatter(1, 2)
    bypass(0)
    rows_forward(0, 2, 1)
    bypass(1)
    rows_forward(1, 2, 1)
    grad_modes(0)
    grad_modes(1)
    rows_back(1, 0, 3)
    weight_grad(0)
    rows_back(1, 1, 3)
    weight_grad(1)

    for phase in range(4):
        for b in range(2):
            sent = send.at[phase, b, pl.ds(0, GROUP - 1)]
            pltpu.make_async_copy(sent, sent, a2a_send.at[phase, b]).wait()
            ref = xr.at[0, b]
            pltpu.make_async_copy(ref, ref, x_send.at[phase, b]).wait()
    if dps > 1:
        for i, ref in enumerate((xb, gb)):
            for b in range(2):
                sent = ref.at[b, pl.ds(0, 512 - per)]
                pltpu.make_async_copy(sent, sent, dp_send.at[i, b]).wait()
    for b in range(2):
        pltpu.make_async_copy(xv.at[b], side.at[b], out_sem.at[b]).wait()
        arrived(b, 3)


def finish(side, lines, col_h, sgrad, out, weights_out, sv, lv, col, gv, side_sem, sem):
    def piece(b, n):
        at = pl.ds(n * 8, 8)
        return pltpu.make_async_copy(side.at[b, at], sv.at[b, at], side_sem.at[b, n])

    pltpu.make_async_copy(col_h, col, sem.at[0]).start()
    for b in range(2):
        for s in range(GROUP):
            pltpu.make_async_copy(lines.at[b, s], lv.at[b, s], sem.at[1 + b]).start()
        for n in range(8):
            piece(b, n).start()
    pltpu.make_async_copy(sgrad, gv, sem.at[3]).start()
    pltpu.make_async_copy(col, col, sem.at[0]).wait()
    for b in range(2):
        pltpu.make_async_copy(lv.at[b], lv.at[b], sem.at[1 + b]).wait()

        def step(n, carry, b=b):
            piece(b, n).wait()
            for i in range(2):
                at = pl.ds(pl.multiple_of(n * 8 + i * 4, 4), 4)
                rows = pl.ds(pl.multiple_of((2 * n + i) * 16, 16), 16)
                part = lv[b, :, rows, :].reshape(128, 128)
                got = dot(part, col[...], TN) + sv[b, at].reshape(128, 512).astype(F32)
                sv[b, at] = got.astype(BF).reshape(4, 32, 512)
            at = pl.ds(n * 8, 8)
            pltpu.make_async_copy(sv.at[b, at], out.at[b, at], sem.at[4 + b]).start()
            return carry

        lax.fori_loop(0, 8, step, 0, unroll=2)
    pltpu.make_async_copy(gv, gv, sem.at[3]).wait()
    away = pltpu.make_async_copy(gv, weights_out, sem.at[6])
    away.start()
    for b in range(2):
        pltpu.make_async_copy(sv.at[b], sv.at[b], sem.at[4 + b]).wait()
    away.wait()


def shards(dps, clips, cotangent, spectral_weight, point_weight, bias):
    col, fwd, inv, perm = [jnp.asarray(t) for t in tables()]
    any_spec = pl.BlockSpec(memory_space=pl.ANY)
    vmem = pl.BlockSpec(memory_space=pltpu.VMEM)
    per = 512 // dps
    dma = pltpu.SemaphoreType.DMA
    grad_shape = jax.ShapeDtypeStruct((64 // dps, 4, 64, 128), F32)
    side, last, sgrad = pl.pallas_call(
        functools.partial(kernel, dps),
        out_shape=(
            jax.ShapeDtypeStruct((2, 64, 32, 512), BF),
            jax.ShapeDtypeStruct((2, GROUP, 256, 128), BF),
            grad_shape,
        ),
        in_specs=[any_spec] * 3 + [vmem] * 2 + [any_spec] * 4,
        out_specs=(any_spec, any_spec, vmem),
        scratch_shapes=[
            pltpu.VMEM((2, 64, 32, 512), BF),
            pltpu.VMEM((2, 64, 32, 512), BF),
            pltpu.VMEM((64, 4, 64, 128), BF),
            pltpu.VMEM((128, 512), BF),
            pltpu.VMEM((1024, 512), BF),
            pltpu.VMEM((512, 2048), BF),
            pltpu.VMEM((512, 512), BF),
            pltpu.VMEM((4, 2, GROUP, 256, 128), BF),
            pltpu.VMEM((3, 2, GROUP, 256, 128), BF),
            pltpu.VMEM((2, 64, 32, 512), F32),
            pltpu.VMEM((2, 64, 32, 512), BF),
            pltpu.VMEM((2, 2, 2, 128, 256), BF),
            pltpu.VMEM((2, 2, 128, 256), BF),
            pltpu.VMEM((2, 2, 2, 128, 256), BF),
            pltpu.VMEM((2, 512, 128), F32),
            pltpu.VMEM((2, 512, 256), BF),
            pltpu.VMEM((2, dps, per, 256), BF),
            pltpu.VMEM((512, 128), F32),
            pltpu.VMEM((2, 512, 128), BF),
            pltpu.VMEM((2, dps, per, 128), BF),
            pltpu.VMEM((2, 512, 128), F32),
            pltpu.VMEM((512, 128), F32),
            pltpu.VMEM((512, 512), BF),
            pltpu.VMEM((512, 512), BF),
            pltpu.VMEM((512, 128), F32),
            dma((7,)),
            dma((2, 8)),
            dma((4, 2)),
            dma((4, 2)),
            dma((4, 2)),
            dma((4, 2)),
            dma((2, 2)),
            dma((2, 2)),
            dma((2,)),
        ],
        compiler_params=pltpu.CompilerParams(
            collective_id=0, has_side_effects=True, vmem_limit_bytes=60 * 1024 * 1024
        ),
        cost_estimate=pl.CostEstimate(
            flops=20_000_000_000, bytes_accessed=20_000_000, transcendentals=4_000_000
        ),
    )(clips, cotangent, spectral_weight, point_weight, bias.reshape(1, 64), col, fwd, inv, perm)
    return pl.pallas_call(
        finish,
        out_shape=(jax.ShapeDtypeStruct((2, 64, 32, 512), BF), grad_shape),
        in_specs=[any_spec] * 4,
        out_specs=(any_spec, any_spec),
        scratch_shapes=[
            pltpu.VMEM((2, 64, 32, 512), BF),
            pltpu.VMEM((2, GROUP, 256, 128), BF),
            pltpu.VMEM((128, 512), BF),
            pltpu.VMEM(grad_shape.shape, F32),
            dma((2, 8)),
            dma((7,)),
        ],
        compiler_params=pltpu.CompilerParams(vmem_limit_bytes=60 * 1024 * 1024),
        cost_estimate=pl.CostEstimate(
            flops=600_000_000, bytes_accessed=10_000_000, transcendentals=0
        ),
    )(side, last, col, sgrad)


def solution(mesh):
    in_specs = (
        P("dp", None, "pencil", None),
        P("dp", None, "pencil", None),
        P(None, "pencil", None, None),
        P(),
        P(),
    )
    out_specs = (P("dp", None, "pencil", None), P("dp", "pencil", None, None))
    return jax.shard_map(
        functools.partial(shards, mesh.shape["dp"]),
        mesh=mesh,
        in_specs=in_specs,
        out_specs=out_specs,
        check_vma=False,
    )
```

time: 113 us -> 91.7 us (0.81)
  Pallas kernels: 107 us -> 90.7 us
  local copies, waits for them, and re-layouts: 5.64 us -> 0 us
    pallas_call x1, Pallas kernels: 107 us -> 84 us  [shards(): pl.pallas_call(functools.partial(kernel, dps), out_shape=(jax.ShapeDtypeS...]
    pallas_call x0 -> x1, Pallas kernels: none -> 6.78 us  [shards(): pl.pallas_call(finish, out_shape=(jax.ShapeDtypeStruct((2, 64, 32, 512),...]
    unnamed x4 -> x0, local copies, waits for them, and re-layouts: 5.64 us -> none
where the time goes in v1:
time: 91.7 us; the launch traced here: 91.5 us
  Pallas kernels  90.7 us (99%)
    pallas_call x1, Pallas kernels, shards(): pl.pallas_call(functools.partial(kernel, dps), out_shape=(jax.ShapeDtypeS...  84 us
    pallas_call x1, Pallas kernels, shards(): pl.pallas_call(finish, out_shape=(jax.ShapeDtypeStruct((2, 64, 32, 512),...  6.78 us

profile of v1, /device:TPU:1, one launch (start us, length us, event | category | flops | bytes accessed | tf_op | source)
XLA Modules:
  0.0 91.5 jit_solution(1523919849032399864)
XLA Ops:
  0.6 84.0 %shard_map.104 = (bf16[2,64,32,512]{3,2,1,0:T(8,128)(2,1)}, bf16[2,8,256,128]{3,2,1,0:T(8,128)(2,1)}, f32[4,4,64,128]{3,2,1,0:T(8,128)}) custom-call(bf16[2,64,32,512]{3,2,1,0:T(8,128)(2,1)} %clips.1, bf16[2,64,32,512]{3,2,1,0:T(8,128)(2,1)} %cot.1, bf16[64,4,64,128]{3,2,1,0:T(8,128)(2,1)} %weight.1, bf16[64,64]{1,0:T(8,128)(2,1)} %pw.1, ...), custom_call_target="tpu_custom_call" | custom-call | flops 20000000000 | bytes 20000000 | tf_op jit(solution)/shard_map/pallas_call | solution.py:486
  84.6 6.8 %shard_map.105 = (bf16[2,64,32,512]{3,2,1,0:T(8,128)(2,1)}, f32[4,4,64,128]{3,2,1,0:T(8,128)}) custom-call(bf16[2,64,32,512]{3,2,1,0:T(8,128)(2,1)} %get-tuple-element.5.side, bf16[2,8,256,128]{3,2,1,0:T(8,128)(2,1)} %get-tuple-element.6.lines, bf16[128,512]{1,0:T(8,128)(2,1)} %constant.8.clone.col_h, f32[4,4,64,128]{3,2,1,0:T(8,128)} %get-tuple-element.7.sgrad), custom_call_target="tpu_custom_call" | custom-call | flops 600000000 | bytes 10000000 | tf_op jit(solution)/shard_map/pallas_call | solution.py:538

commit v2 on v1

--- a/solution.py
+++ b/solution.py
@@ -67,9 +67,9 @@
     clips, cot, weight, pw, bias, col_h, fwd_h, inv_h, perm_h,
     side, last, sgrad,
     xv, cv, wv, col, fwd, inv, perm,
-    send, recv, zs, dz, xp, xr, ya,
+    send, recv, relay, zs, dz, xp, xr, ya,
     xbf, xb, xbr, gbf, gb, gbr, dd, y3, kf, kb, bcol,
-    in_sem, clip_sem, a2a_send, a2a_recv, x_send, x_recv, dp_send, dp_recv, out_sem,
+    in_sem, clip_sem, a2a_send, a2a_recv, relay_send, relay_recv, x_send, x_recv, dp_send, dp_recv, out_sem,
 ):
     pen = lax.axis_index("pencil")
     dpi = lax.axis_index("dp")
@@ -133,15 +133,35 @@
 
         lax.fori_loop(0, 8, step, 0, unroll=2)
 
-    def send_one(b, phase, to):
+    def send_one(b, phase, dy, dc):
+        to = peer_of(dy, dc)
+        if dy == 2:
+            dst, via = relay.at[phase, b, dc], peer_of((1, 3)[dc], 0)
+            sems = relay_send.at[phase, b], relay_recv.at[phase, b, dc]
+        else:
+            dst, via = slots(b, phase).at[me], to
+            sems = a2a_send.at[phase, b], a2a_recv.at[phase, b]
         pltpu.make_async_remote_copy(
             src_ref=send.at[phase, b, to],
-            dst_ref=slots(b, phase).at[me],
-            send_sem=a2a_send.at[phase, b],
-            recv_sem=a2a_recv.at[phase, b],
-            device_id={"pencil": half * GROUP + to},
+            dst_ref=dst,
+            send_sem=sems[0],
+            recv_sem=sems[1],
+            device_id={"pencil": half * GROUP + via},
             device_id_type=MESH,
         ).start()
+
+    def forward(b, phase):
+        for dc in range(2):
+            ref = relay.at[phase, b, dc]
+            pltpu.make_async_copy(ref, ref, relay_recv.at[phase, b, dc]).wait()
+            pltpu.make_async_remote_copy(
+                src_ref=ref,
+                dst_ref=slots(b, phase).at[peer_of((3, 1)[dc], 0)],
+                send_sem=a2a_send.at[phase, b],
+                recv_sem=a2a_recv.at[phase, b],
+                device_id={"pencil": half * GROUP + peer_of((1, 3)[dc], dc)},
+                device_id_type=MESH,
+            ).start()
 
     def keep_own(b, phase):
         pltpu.make_async_copy(
@@ -150,7 +170,7 @@
 
     def scatter(b, phase):
         for dy, dc in PEERS:
-            send_one(b, phase, peer_of(dy, dc))
+            send_one(b, phase, dy, dc)
         keep_own(b, phase)
 
     def arrived(b, phase):
@@ -230,7 +250,7 @@
             if (dy, dc) == (0, 0):
                 keep_own(b, phase)
             else:
-                send_one(b, phase, to)
+                send_one(b, phase, dy, dc)
 
     def mix_points(values, b, matrix, add, tiles=(0, 2)):
         def step(t, carry):
@@ -346,8 +366,11 @@
 
         lax.fori_loop(*chunks, step, 0, unroll=4)
 
-    def bypass(b):
-        mix_points(dz, b, kb, None)
+    def bypass(b, between=None):
+        mix_points(dz, b, kb, None, (0, 1))
+        if between is not None:
+            between()
+        mix_points(dz, b, kb, None, (1, 2))
         pltpu.make_async_copy(xv.at[b], side.at[b], out_sem.at[b]).start()
 
     def weight_grad(b):
@@ -372,6 +395,7 @@
     fwd_wait = load(fwd_h.at[half], fwd, 4, 1)
     perm_wait = load(perm_h, perm, 2, 2)
     columns(xv, 1, 0)
+    forward(0, 0)
     scatter(1, 0)
     weight_wait = load(weight, wv, 16, 3)
     inv_wait = load(inv_h.at[half], inv, 4, 4)
@@ -388,6 +412,7 @@
     kb[...] = jnp.where(same, dot(dot(spread, pw[...]).astype(BF), spread, NT), 0.0).astype(BF)
     biased = (spread.astype(F32) * bias[...].astype(F32)).astype(BF)
     bcol[...] = dot(biased, jnp.ones((64, 128), BF))
+    forward(1, 0)
     mix_points(xv, 0, kf, bcol)
 
     fwd_wait()
@@ -401,6 +426,8 @@
     inv_wait()
     rows_back(0, 0, 1)
     rows_back(0, 1, 1)
+    forward(0, 1)
+    forward(1, 1)
 
     arrived(0, 1)
     cot_waits[0]()
@@ -409,10 +436,12 @@
     scatter(0, 2)
     arrived(1, 1)
     cot_waits[1]()
-    activation(1, (0, 16))
+    activation(1, (0, 4))
+    forward(0, 2)
+    activation(1, (4, 16))
     columns(dz, 1, 2)
     scatter(1, 2)
-    bypass(0)
+    bypass(0, lambda: forward(1, 2))
     rows_forward(0, 2, 1)
     bypass(1)
     rows_forward(1, 2, 1)
@@ -420,13 +449,17 @@
     grad_modes(1)
     rows_back(1, 0, 3)
     weight_grad(0)
+    forward(0, 3)
     rows_back(1, 1, 3)
     weight_grad(1)
+    forward(1, 3)
 
     for phase in range(4):
         for b in range(2):
             sent = send.at[phase, b, pl.ds(0, GROUP - 1)]
             pltpu.make_async_copy(sent, sent, a2a_send.at[phase, b]).wait()
+            sent = relay.at[phase, b]
+            pltpu.make_async_copy(sent, sent, relay_send.at[phase, b]).wait()
             ref = xr.at[0, b]
             pltpu.make_async_copy(ref, ref, x_send.at[phase, b]).wait()
     if dps > 1:
@@ -502,6 +535,7 @@
             pltpu.VMEM((512, 512), BF),
             pltpu.VMEM((4, 2, GROUP, 256, 128), BF),
             pltpu.VMEM((3, 2, GROUP, 256, 128), BF),
+            pltpu.VMEM((4, 2, 2, 256, 128), BF),
             pltpu.VMEM((2, 64, 32, 512), F32),
             pltpu.VMEM((2, 64, 32, 512), BF),
             pltpu.VMEM((2, 2, 2, 128, 256), BF),
@@ -522,6 +556,8 @@
             dma((2, 8)),
             dma((4, 2)),
             dma((4, 2)),
+            dma((4, 2)),
+            dma((4, 2, 2)),
             dma((4, 2)),
             dma((4, 2)),
             dma((2, 2)),

time: 91.7 us -> 102 us (1.11)
  Pallas kernels: 90.7 us -> 101 us
    pallas_call x1, Pallas kernels: 84 us -> 94.1 us  [shards(): pl.pallas_call(functools.partial(kernel, dps), out_shape=(jax.ShapeDtypeS...]
where the time goes in v2:
time: 102 us
  Pallas kernels  101 us (99%)
    pallas_call x1, Pallas kernels, shards(): pl.pallas_call(functools.partial(kernel, dps), out_shape=(jax.ShapeDtypeS...  94.1 us
    pallas_call x1, Pallas kernels, shards(): pl.pallas_call(finish, out_shape=(jax.ShapeDtypeStruct((2, 64, 32, 512),...  6.78 us

profile of v2, /device:TPU:1, one launch (start us, length us, event | category | flops | bytes accessed | tf_op | source)
XLA Modules:
  0.0 101.7 jit_solution(2952068245650956021)
XLA Ops:
  0.6 94.1 %shard_map.104 = (bf16[2,64,32,512]{3,2,1,0:T(8,128)(2,1)}, bf16[2,8,256,128]{3,2,1,0:T(8,128)(2,1)}, f32[4,4,64,128]{3,2,1,0:T(8,128)}) custom-call(bf16[2,64,32,512]{3,2,1,0:T(8,128)(2,1)} %clips.1, bf16[2,64,32,512]{3,2,1,0:T(8,128)(2,1)} %cot.1, bf16[64,4,64,128]{3,2,1,0:T(8,128)(2,1)} %weight.1, bf16[64,64]{1,0:T(8,128)(2,1)} %pw.1, ...), custom_call_target="tpu_custom_call" | custom-call | flops 20000000000 | bytes 20000000 | tf_op jit(solution)/shard_map/pallas_call | solution.py:519
  94.7 6.8 %shard_map.105 = (bf16[2,64,32,512]{3,2,1,0:T(8,128)(2,1)}, f32[4,4,64,128]{3,2,1,0:T(8,128)}) custom-call(bf16[2,64,32,512]{3,2,1,0:T(8,128)(2,1)} %get-tuple-element.5.side, bf16[2,8,256,128]{3,2,1,0:T(8,128)(2,1)} %get-tuple-element.6.lines, bf16[128,512]{1,0:T(8,128)(2,1)} %constant.8.clone.col_h, f32[4,4,64,128]{3,2,1,0:T(8,128)} %get-tuple-element.7.sgrad), custom_call_target="tpu_custom_call" | custom-call | flops 600000000 | bytes 10000000 | tf_op jit(solution)/shard_map/pallas_call | solution.py:574

commit v3 on v1

--- a/solution.py
+++ b/solution.py
@@ -117,7 +117,7 @@
     sign = jnp.where(low, 1.0, -1.0).astype(F32)
 
     def slots(b, phase):
-        return recv.at[phase, b] if phase < 3 else last.at[b]
+        return last if (phase, b) == (3, 1) else recv.at[phase, b]
 
     def columns(values, b, phase):
         def step(n, carry):
@@ -161,11 +161,13 @@
         arrived(b, phase)
         lhs = jnp.concatenate([recv[phase, b, s] for s in range(GROUP)], axis=1)
         pieces = []
-        for c4 in range(4):
-            part = dot(lhs, fwd[:, c4 * 128 : (c4 + 1) * 128]).reshape(16, 2, 8, 128)
-            cosine = part[:, 0].reshape(128, 128)
-            sine = part[:, 1].reshape(128, 128)
-            pieces.append((cosine * sign - pltpu.roll(sine, 64, 1)).astype(BF))
+        for n in range(2):
+            wide = dot(lhs, fwd[:, n * 256 : (n + 1) * 256])
+            for i in range(2):
+                part = wide[:, i * 128 : (i + 1) * 128].reshape(16, 2, 8, 128)
+                cosine = part[:, 0].reshape(128, 128)
+                sine = part[:, 1].reshape(128, 128)
+                pieces.append((cosine * sign - pltpu.roll(sine, 64, 1)).astype(BF))
         spec = dot(jnp.concatenate(pieces, axis=0), perm[...], TN).astype(BF)
         xp[which, b, 0] = spec[:, :256]
         xp[which, b, 1] = spec[:, 256:]
@@ -185,17 +187,14 @@
         x_wait(which, b, xr.at[which, b])
         return xp[which, b, half].astype(F32) + xr[which, b].astype(F32)
 
-    def to_owner(src, dst, i, b):
-        def rows_of(d):
-            return src.at[b, pl.ds(pl.multiple_of(d * per, per), per)]
-
+    def to_owner(src, dst, i):
         def step(r, carry):
             to = (dpi + r) % dps
             pltpu.make_async_remote_copy(
-                src_ref=rows_of(to),
-                dst_ref=dst.at[b, dpi],
-                send_sem=dp_send.at[i, b],
-                recv_sem=dp_recv.at[i, b],
+                src_ref=src.at[to],
+                dst_ref=dst.at[dpi],
+                send_sem=dp_send.at[i],
+                recv_sem=dp_recv.at[i],
                 device_id={"dp": to},
                 device_id_type=MESH,
             ).start()
@@ -203,7 +202,7 @@
 
         if dps > 1:
             lax.fori_loop(1, dps, step, 0)
-        pltpu.make_async_copy(rows_of(dpi), dst.at[b, dpi], dp_recv.at[i, b]).start()
+        pltpu.make_async_copy(src.at[dpi], dst.at[dpi], dp_recv.at[i]).start()
 
     def give_partner(i, b):
         pltpu.make_async_remote_copy(
@@ -257,20 +256,23 @@
     scale = jnp.where(pen == 0, 1.0, 2.0).astype(F32) / 262144.0
     scale_lane = jnp.where(jnp.logical_and(low, pen == 0), 1.0, 2.0).astype(F32) / 262144.0
 
+    pairs = kper // 2
+
+    def own_rows(pair):
+        return pl.ds(pl.multiple_of(pair % pairs * 16, 16), 16)
+
     def mix_modes(b):
         spec = spectrum(0, b)
         for ri in range(2):
             for j in range(4):
                 for p in range(2):
-                    if p == j // 2:
-                        part = spec[ri * 64 : (ri + 1) * 64, p * 128 : (p + 1) * 128]
-                        part = jnp.where(low if j % 2 == 0 else jnp.logical_not(low), part, 0.0)
-                    else:
-                        part = jnp.zeros((64, 128), F32)
+                    if p != j // 2:
+                        continue
+                    part = spec[ri * 64 : (ri + 1) * 64, p * 128 : (p + 1) * 128]
+                    part = jnp.where(low if j % 2 == 0 else jnp.logical_not(low), part, 0.0)
                     xbf[p, pl.ds(ri * 4 + j, 64, stride=8), :] = part
         for p in range(2):
-            xb[b, :, p * 128 : (p + 1) * 128] = xbf[p].astype(BF)
-        to_owner(xb, xbr, 0, b)
+            xb[:, b, :, p * 128 : (p + 1) * 128] = xbf[p].astype(BF).reshape(dps, per, 128)
 
         def step(n, carry):
             for i in range(8):
@@ -279,7 +281,7 @@
                 both = jnp.concatenate(
                     [wv[2 * pair].reshape(256, 128), wv[2 * pair + 1].reshape(256, 128)], axis=1
                 )
-                got = dot(xb[b, pl.ds(at, 16), :], both)
+                got = dot(xb[pair // pairs, b, own_rows(pair), :], both)
                 y3[pl.ds(at, 8), :] = got[:8, :128]
                 y3[pl.ds(at + 8, 8), :] = got[8:, 128:]
             return carry
@@ -312,14 +314,14 @@
             ):
                 gbf[pl.ds(2 * p + i, 64, stride=8), :] = re
                 gbf[pl.ds(4 + 2 * p + i, 64, stride=8), :] = im * sign
-        gb[b] = gbf[...].astype(BF)
-        to_owner(gb, gbr, 1, b)
+        gb[:, b] = gbf[...].astype(BF).reshape(dps, per, 128)
 
         def step(n, carry):
             for i in range(8):
                 pair = n * 8 + i
                 at = pl.multiple_of(pair * 16, 16)
-                got = dot(gb[b, pl.ds(at, 16), :], wv[pl.ds(2 * pair, 2)].reshape(512, 128), NT)
+                rhs = wv[pl.ds(2 * pair, 2)].reshape(512, 128)
+                got = dot(gb[pair // pairs, b, own_rows(pair), :], rhs, NT)
                 for p in range(2):
                     dd[p, pl.ds(at, 8), :] = got[:8, p * 128 : (p + 1) * 128]
                     dd[p, pl.ds(at + 8, 8), :] = got[8:, 256 + p * 128 : 384 + p * 128]
@@ -346,24 +348,35 @@
 
         lax.fori_loop(*chunks, step, 0, unroll=4)
 
-    def bypass(b):
-        mix_points(dz, b, kb, None)
+    def leave(b):
         pltpu.make_async_copy(xv.at[b], side.at[b], out_sem.at[b]).start()
 
-    def weight_grad(b):
+    def finish_first():
+        arrived(0, 3)
+
+        def step(n, carry):
+            at = pl.ds(pl.multiple_of(n * 4, 4), 4)
+            lines = recv[3, 0, :, pl.ds(pl.multiple_of(n * 16, 16), 16), :].reshape(128, 128)
+            got = dot(lines, col[...], TN) + xv[0, at].reshape(128, 512).astype(F32)
+            xv[0, at] = got.astype(BF).reshape(4, 32, 512)
+            return carry
+
+        lax.fori_loop(0, 16, step, 0, unroll=4)
+        leave(0)
+
+    def weight_grad():
         for i, ref in enumerate((xbr, gbr)):
-            pltpu.make_async_copy(ref.at[b], ref.at[b], dp_recv.at[i, b]).wait()
+            pltpu.make_async_copy(ref, ref, dp_recv.at[i]).wait()
         first_rows = jnp.where(row16 < 8, 1.0, 0.0).astype(F32)
-        for pair in range(kper // 2):
+        for pair in range(pairs):
             at = slice(pair * 16, (pair + 1) * 16)
-            left = xbr[b, :, at, :].reshape(dps * 16, 256)
-            right = gbr[b, :, at, :].astype(F32)
-            head = (right * first_rows).astype(BF).reshape(dps * 16, 128)
-            tail = (right * (1.0 - first_rows)).astype(BF).reshape(dps * 16, 128)
+            left = xbr[:, :, at, :].reshape(2 * dps * 16, 256)
+            right = gbr[:, :, at, :].astype(F32)
+            head = (right * first_rows).astype(BF).reshape(2 * dps * 16, 128)
+            tail = (right * (1.0 - first_rows)).astype(BF).reshape(2 * dps * 16, 128)
             got = dot(left, jnp.concatenate([head, tail], axis=1), TN)
             for i in range(2):
-                part = got[:, i * 128 : (i + 1) * 128].reshape(4, 64, 128)
-                sgrad[2 * pair + i] = part if b == 0 else sgrad[2 * pair + i] + part
+                sgrad[2 * pair + i] = got[:, i * 128 : (i + 1) * 128].reshape(4, 64, 128)
 
     col_wait()
     columns(xv, 0, 0)
@@ -384,6 +397,8 @@
         lax.broadcasted_iota(jnp.int32, (512, 512), 0) % 8
         == lax.broadcasted_iota(jnp.int32, (512, 512), 1) % 8
     )
+    for p in range(2):
+        xbf[p] = jnp.zeros((512, 128), F32)
     kf[...] = jnp.where(same, dot(dot(spread, pw[...], NT).astype(BF), spread, NT), 0.0).astype(BF)
     kb[...] = jnp.where(same, dot(dot(spread, pw[...]).astype(BF), spread, NT), 0.0).astype(BF)
     biased = (spread.astype(F32) * bias[...].astype(F32)).astype(BF)
@@ -400,28 +415,27 @@
     mix_modes(1)
     inv_wait()
     rows_back(0, 0, 1)
+    to_owner(xb, xbr, 0)
     rows_back(0, 1, 1)
 
-    arrived(0, 1)
-    cot_waits[0]()
-    activation(0, (0, 16))
-    columns(dz, 0, 2)
-    scatter(0, 2)
-    arrived(1, 1)
-    cot_waits[1]()
-    activation(1, (0, 16))
-    columns(dz, 1, 2)
-    scatter(1, 2)
-    bypass(0)
+    for b in range(2):
+        arrived(b, 1)
+        cot_waits[b]()
+        activation(b, (0, 16))
+        columns(dz, b, 2)
+        scatter(b, 2)
     rows_forward(0, 2, 1)
-    bypass(1)
+    mix_points(dz, 0, kb, None)
+    mix_points(dz, 1, kb, None)
+    leave(1)
     rows_forward(1, 2, 1)
     grad_modes(0)
     grad_modes(1)
     rows_back(1, 0, 3)
-    weight_grad(0)
+    to_owner(gb, gbr, 1)
     rows_back(1, 1, 3)
-    weight_grad(1)
+    finish_first()
+    weight_grad()
 
     for phase in range(4):
         for b in range(2):
@@ -431,12 +445,11 @@
             pltpu.make_async_copy(ref, ref, x_send.at[phase, b]).wait()
     if dps > 1:
         for i, ref in enumerate((xb, gb)):
-            for b in range(2):
-                sent = ref.at[b, pl.ds(0, 512 - per)]
-                pltpu.make_async_copy(sent, sent, dp_send.at[i, b]).wait()
+            sent = ref.at[pl.ds(0, dps - 1)]
+            pltpu.make_async_copy(sent, sent, dp_send.at[i]).wait()
     for b in range(2):
         pltpu.make_async_copy(xv.at[b], side.at[b], out_sem.at[b]).wait()
-        arrived(b, 3)
+    arrived(1, 3)
 
 
 def finish(side, lines, col_h, sgrad, out, weights_out, sv, lv, col, gv, side_sem, sem):
@@ -444,35 +457,39 @@
         at = pl.ds(n * 8, 8)
         return pltpu.make_async_copy(side.at[b, at], sv.at[b, at], side_sem.at[b, n])
 
+    def write(b, n):
+        at = pl.ds(n * 8, 8)
+        pltpu.make_async_copy(sv.at[b, at], out.at[b, at], sem.at[3 + b]).start()
+
     pltpu.make_async_copy(col_h, col, sem.at[0]).start()
-    for b in range(2):
-        for s in range(GROUP):
-            pltpu.make_async_copy(lines.at[b, s], lv.at[b, s], sem.at[1 + b]).start()
+    for s in range(GROUP):
+        pltpu.make_async_copy(lines.at[s], lv.at[s], sem.at[1]).start()
+    for b in (1, 0):
         for n in range(8):
             piece(b, n).start()
-    pltpu.make_async_copy(sgrad, gv, sem.at[3]).start()
+    pltpu.make_async_copy(sgrad, gv, sem.at[2]).start()
     pltpu.make_async_copy(col, col, sem.at[0]).wait()
-    for b in range(2):
-        pltpu.make_async_copy(lv.at[b], lv.at[b], sem.at[1 + b]).wait()
-
-        def step(n, carry, b=b):
-            piece(b, n).wait()
-            for i in range(2):
-                at = pl.ds(pl.multiple_of(n * 8 + i * 4, 4), 4)
-                rows = pl.ds(pl.multiple_of((2 * n + i) * 16, 16), 16)
-                part = lv[b, :, rows, :].reshape(128, 128)
-                got = dot(part, col[...], TN) + sv[b, at].reshape(128, 512).astype(F32)
-                sv[b, at] = got.astype(BF).reshape(4, 32, 512)
-            at = pl.ds(n * 8, 8)
-            pltpu.make_async_copy(sv.at[b, at], out.at[b, at], sem.at[4 + b]).start()
-            return carry
-
-        lax.fori_loop(0, 8, step, 0, unroll=2)
-    pltpu.make_async_copy(gv, gv, sem.at[3]).wait()
-    away = pltpu.make_async_copy(gv, weights_out, sem.at[6])
+    pltpu.make_async_copy(lv, lv, sem.at[1]).wait()
+
+    def step(n, carry):
+        piece(1, n).wait()
+        for i in range(2):
+            at = pl.ds(pl.multiple_of(n * 8 + i * 4, 4), 4)
+            rows = pl.ds(pl.multiple_of((2 * n + i) * 16, 16), 16)
+            part = lv[:, rows, :].reshape(128, 128)
+            got = dot(part, col[...], TN) + sv[1, at].reshape(128, 512).astype(F32)
+            sv[1, at] = got.astype(BF).reshape(4, 32, 512)
+        write(1, n)
+        piece(0, n).wait()
+        write(0, n)
+        return carry
+
+    lax.fori_loop(0, 8, step, 0, unroll=2)
+    pltpu.make_async_copy(gv, gv, sem.at[2]).wait()
+    away = pltpu.make_async_copy(gv, weights_out, sem.at[5])
     away.start()
     for b in range(2):
-        pltpu.make_async_copy(sv.at[b], sv.at[b], sem.at[4 + b]).wait()
+        pltpu.make_async_copy(sv.at[b], sv.at[b], sem.at[3 + b]).wait()
     away.wait()
 
 
@@ -487,7 +504,7 @@
         functools.partial(kernel, dps),
         out_shape=(
             jax.ShapeDtypeStruct((2, 64, 32, 512), BF),
-            jax.ShapeDtypeStruct((2, GROUP, 256, 128), BF),
+            jax.ShapeDtypeStruct((GROUP, 256, 128), BF),
             grad_shape,
         ),
         in_specs=[any_spec] * 3 + [vmem] * 2 + [any_spec] * 4,
@@ -501,18 +518,18 @@
             pltpu.VMEM((512, 2048), BF),
             pltpu.VMEM((512, 512), BF),
             pltpu.VMEM((4, 2, GROUP, 256, 128), BF),
-            pltpu.VMEM((3, 2, GROUP, 256, 128), BF),
+            pltpu.VMEM((4, 2, GROUP, 256, 128), BF),
             pltpu.VMEM((2, 64, 32, 512), F32),
             pltpu.VMEM((2, 64, 32, 512), BF),
             pltpu.VMEM((2, 2, 2, 128, 256), BF),
             pltpu.VMEM((2, 2, 128, 256), BF),
             pltpu.VMEM((2, 2, 2, 128, 256), BF),
             pltpu.VMEM((2, 512, 128), F32),
-            pltpu.VMEM((2, 512, 256), BF),
-            pltpu.VMEM((2, dps, per, 256), BF),
+            pltpu.VMEM((dps, 2, per, 256), BF),
+            pltpu.VMEM((dps, 2, per, 256), BF),
             pltpu.VMEM((512, 128), F32),
-            pltpu.VMEM((2, 512, 128), BF),
-            pltpu.VMEM((2, dps, per, 128), BF),
+            pltpu.VMEM((dps, 2, per, 128), BF),
+            pltpu.VMEM((dps, 2, per, 128), BF),
             pltpu.VMEM((2, 512, 128), F32),
             pltpu.VMEM((512, 128), F32),
             pltpu.VMEM((512, 512), BF),
@@ -524,8 +541,8 @@
             dma((4, 2)),
             dma((4, 2)),
             dma((4, 2)),
-            dma((2, 2)),
-            dma((2, 2)),
+            dma((2,)),
+            dma((2,)),
             dma((2,)),
         ],
         compiler_params=pltpu.CompilerParams(
@@ -542,11 +559,11 @@
         out_specs=(any_spec, any_spec),
         scratch_shapes=[
             pltpu.VMEM((2, 64, 32, 512), BF),
-            pltpu.VMEM((2, GROUP, 256, 128), BF),
+            pltpu.VMEM((GROUP, 256, 128), BF),
             pltpu.VMEM((128, 512), BF),
             pltpu.VMEM(grad_shape.shape, F32),
             dma((2, 8)),
-            dma((7,)),
+            dma((6,)),
         ],
         compiler_params=pltpu.CompilerParams(vmem_limit_bytes=60 * 1024 * 1024),
         cost_estimate=pl.CostEstimate(

time: 91.7 us -> 88.2 us (0.962)
  Pallas kernels: 90.7 us -> 87.4 us
    pallas_call x1, Pallas kernels: 84 us -> 82 us  [shards(): pl.pallas_call(functools.partial(kernel, dps), out_shape=(jax.ShapeDtypeS...]
    pallas_call x1, Pallas kernels: 6.78 us -> 5.36 us  [shards(): pl.pallas_call(finish, out_shape=(jax.ShapeDtypeStruct((2, 64, 32, 512),...]
where the time goes in v3:
time: 88.2 us; the launch traced here: 88 us
  Pallas kernels  87.4 us (99%)
    pallas_call x1, Pallas kernels, shards(): pl.pallas_call(functools.partial(kernel, dps), out_shape=(jax.ShapeDtypeS...  82 us
    pallas_call x1, Pallas kernels, shards(): pl.pallas_call(finish, out_shape=(jax.ShapeDtypeStruct((2, 64, 32, 512),...  5.36 us

profile of v3, /device:TPU:1, one launch (start us, length us, event | category | flops | bytes accessed | tf_op | source)
XLA Modules:
  0.0 88.0 jit_solution(3744943376343188578)
XLA Ops:
  0.6 82.0 %shard_map.104 = (bf16[2,64,32,512]{3,2,1,0:T(8,128)(2,1)}, bf16[8,256,128]{2,1,0:T(8,128)(2,1)}, f32[4,4,64,128]{3,2,1,0:T(8,128)}) custom-call(bf16[2,64,32,512]{3,2,1,0:T(8,128)(2,1)} %clips.1, bf16[2,64,32,512]{3,2,1,0:T(8,128)(2,1)} %cot.1, bf16[64,4,64,128]{3,2,1,0:T(8,128)(2,1)} %weight.1, bf16[64,64]{1,0:T(8,128)(2,1)} %pw.1, bf16[1,64]{1,0:T(2,128)(2,1)} %bitcast.1, ...), custom_call_target="tpu_custom_call" | custom-call | flops 20000000000 | bytes 20000000 | tf_op jit(solution)/shard_map/pallas_call | solution.py:503
  82.7 5.4 %shard_map.105 = (bf16[2,64,32,512]{3,2,1,0:T(8,128)(2,1)}, f32[4,4,64,128]{3,2,1,0:T(8,128)}) custom-call(bf16[2,64,32,512]{3,2,1,0:T(8,128)(2,1)} %get-tuple-element.5.side, bf16[8,256,128]{2,1,0:T(8,128)(2,1)} %get-tuple-element.6.lines, bf16[128,512]{1,0:T(8,128)(2,1)} %constant.8.clone.col_h, f32[4,4,64,128]{3,2,1,0:T(8,128)} %get-tuple-element.7.sgrad), custom_call_target="tpu_custom_call" | custom-call | flops 600000000 | bytes 10000000 | tf_op jit(solution)/shard_map/pallas_call | solution.py:555

commit v4 on v3

--- a/solution.py
+++ b/solution.py
@@ -14,7 +14,7 @@
 MESH = pl.DeviceIdType.MESH
 BF = jnp.bfloat16
 F32 = jnp.float32
-GROUP = 8
+GROUP = 16
 TN = (((0,), (0,)), ((), ()))
 NT = (((1,), (1,)), ((), ()))
 NN = (((1,), (0,)), ((), ()))
@@ -26,8 +26,7 @@
 
 def tables():
     w = np.arange(512)
-    g, half, j4 = np.meshgrid(np.arange(8), np.arange(2), np.arange(4), indexing="ij")
-    j = ((half * 8 + g) * 4 + j4).reshape(8, 8)
+    j = np.arange(64).reshape(16, 4)
     phase = (j[:, :, None] * w % 512) * (TWO_PI / 512)
     col = np.stack([np.cos(phase), np.sin(phase)], axis=1).reshape(128, 512)
     k = np.arange(64)
@@ -35,14 +34,15 @@
     h = np.arange(512)
     phase = (h[:, None] * f[None, :] % 512) * (TWO_PI / 512)
     ca, sa = np.cos(phase), np.sin(phase)
-    r = np.stack([ca, sa], axis=1).reshape(2, 8, 32, 128)
+    r = np.stack([ca, sa], axis=1).reshape(16, 32, 128)
     eye = np.eye(4)
-    fwd = np.einsum("xshn,cd->xschdn", r, eye).reshape(2, 1024, 512)
+    fwd = np.einsum("shn,cd->schdn", r, eye).reshape(2048, 512)
     first = np.stack([ca, -sa], axis=1)
     second = np.stack([-sa, -ca], axis=1)
-    inv = np.stack([first, second], axis=1).reshape(2, 8, 32, 2, 128)
-    inv = np.einsum("xshqn,cd->xcnsqdh", inv, eye).reshape(2, 512, 2048)
-    perm = np.einsum("ad,be,cf->abcfed", np.eye(4), np.eye(16), np.eye(8)).reshape(512, 512)
+    inv = np.stack([first, second], axis=1).reshape(16, 32, 2, 128)
+    inv = np.einsum("shqn,cd->cnsqdh", inv, eye).reshape(512, 4096)
+    perm = np.einsum("ad,be,cf,t->abtcfed", np.eye(4), np.eye(16), np.eye(4), np.ones(2))
+    perm = perm.reshape(512, 256)
     return [np.asarray(t, np.float32).astype(ml_dtypes.bfloat16) for t in (col, fwd, inv, perm)]
 
 
@@ -59,7 +59,7 @@
     return jnp.where(z >= 0.0, 1.0 - q, q)
 
 
-PEERS = ((2, 0), (2, 1), (1, 0), (3, 0), (1, 1), (3, 1), (0, 1))
+PEERS = tuple((dx, dy, dc) for dx in (1, 0) for dy in (2, 1, 3, 0) for dc in (1, 0))[:-1]
 
 
 def kernel(
@@ -67,16 +67,12 @@
     clips, cot, weight, pw, bias, col_h, fwd_h, inv_h, perm_h,
     side, last, sgrad,
     xv, cv, wv, col, fwd, inv, perm,
-    send, recv, zs, dz, xp, xr, ya,
+    send, recv, zs, dz, ya,
     xbf, xb, xbr, gbf, gb, gbr, dd, y3, kf, kb, bcol,
-    in_sem, clip_sem, a2a_send, a2a_recv, x_send, x_recv, dp_send, dp_recv, out_sem,
+    in_sem, clip_sem, a2a_send, a2a_recv, dp_send, dp_recv, out_sem,
 ):
     pen = lax.axis_index("pencil")
     dpi = lax.axis_index("dp")
-    half = pen // GROUP
-    me = pen % GROUP
-    other = 1 - half
-    partner = other * GROUP + me
     per = 512 // dps
     kper = 64 // dps
 
@@ -96,14 +92,13 @@
         for n in range(8):
             clip_piece(b, n).start()
 
-    def peer_of(dy, dc):
-        return (me // 2 + dy) % 4 * 2 + (me % 2 + dc) % 2
+    def peer_of(dx, dy, dc):
+        return (pen // 8 + dx) % 2 * 8 + (pen // 2 + dy) % 4 * 2 + (pen + dc) % 2
 
     barrier = pltpu.get_barrier_semaphore()
-    for dy, dc in PEERS:
-        peer = half * GROUP + peer_of(dy, dc)
-        pl.semaphore_signal(barrier, inc=1, device_id={"pencil": peer}, device_id_type=MESH)
-    pl.semaphore_signal(barrier, inc=1, device_id={"pencil": partner}, device_id_type=MESH)
+    for steps in PEERS:
+        peer = {"pencil": peer_of(*steps)}
+        pl.semaphore_signal(barrier, inc=1, device_id=peer, device_id_type=MESH)
 
     def greet_dp(r, carry):
         pl.semaphore_signal(barrier, inc=1, device_id={"dp": (dpi + r) % dps}, device_id_type=MESH)
@@ -125,10 +120,9 @@
                 clip_piece(b, n).wait()
             rows = values[b, pl.ds(pl.multiple_of(n * 8, 8), 8)].reshape(256, 512)
             part = dot(col[...], rows, NT)
-            for i in range(2):
-                piece = part[:, i * 128 : (i + 1) * 128].reshape(8, 16, 128).astype(BF)
-                at = pl.multiple_of((2 * n + i) * 16, 16)
-                send[phase, b, :, pl.ds(at, 16), :] = piece
+            pieces = [part[:, i * 128 : (i + 1) * 128].reshape(GROUP, 8, 128) for i in range(2)]
+            at = pl.ds(pl.multiple_of(n * 16, 16), 16)
+            send[phase, b, :, at, :] = jnp.concatenate(pieces, axis=1).astype(BF)
             return carry
 
         lax.fori_loop(0, 8, step, 0, unroll=2)
@@ -136,56 +130,39 @@
     def send_one(b, phase, to):
         pltpu.make_async_remote_copy(
             src_ref=send.at[phase, b, to],
-            dst_ref=slots(b, phase).at[me],
+            dst_ref=slots(b, phase).at[pen],
             send_sem=a2a_send.at[phase, b],
             recv_sem=a2a_recv.at[phase, b],
-            device_id={"pencil": half * GROUP + to},
+            device_id={"pencil": to},
             device_id_type=MESH,
         ).start()
 
     def keep_own(b, phase):
         pltpu.make_async_copy(
-            send.at[phase, b, me], slots(b, phase).at[me], a2a_recv.at[phase, b]
+            send.at[phase, b, pen], slots(b, phase).at[pen], a2a_recv.at[phase, b]
         ).start()
 
     def scatter(b, phase):
-        for dy, dc in PEERS:
-            send_one(b, phase, peer_of(dy, dc))
+        for steps in PEERS:
+            send_one(b, phase, peer_of(*steps))
         keep_own(b, phase)
 
     def arrived(b, phase):
         whole = slots(b, phase)
         pltpu.make_async_copy(whole, whole, a2a_recv.at[phase, b]).wait()
 
-    def rows_forward(b, phase, which):
+    def spectrum(b, phase):
         arrived(b, phase)
         lhs = jnp.concatenate([recv[phase, b, s] for s in range(GROUP)], axis=1)
+        upper = lax.broadcasted_iota(jnp.int32, (128, 128), 0) % 8 < 4
         pieces = []
         for n in range(2):
             wide = dot(lhs, fwd[:, n * 256 : (n + 1) * 256])
             for i in range(2):
-                part = wide[:, i * 128 : (i + 1) * 128].reshape(16, 2, 8, 128)
-                cosine = part[:, 0].reshape(128, 128)
-                sine = part[:, 1].reshape(128, 128)
-                pieces.append((cosine * sign - pltpu.roll(sine, 64, 1)).astype(BF))
-        spec = dot(jnp.concatenate(pieces, axis=0), perm[...], TN).astype(BF)
-        xp[which, b, 0] = spec[:, :256]
-        xp[which, b, 1] = spec[:, 256:]
-        pltpu.make_async_remote_copy(
-            src_ref=xp.at[which, b, other],
-            dst_ref=xr.at[which, b],
-            send_sem=x_send.at[which, b],
-            recv_sem=x_recv.at[which, b],
-            device_id={"pencil": partner},
-            device_id_type=MESH,
-        ).start()
-
-    def x_wait(which, b, ref):
-        pltpu.make_async_copy(ref, ref, x_recv.at[which, b]).wait()
-
-    def spectrum(which, b):
-        x_wait(which, b, xr.at[which, b])
-        return xp[which, b, half].astype(F32) + xr[which, b].astype(F32)
+                part = wide[:, i * 128 : (i + 1) * 128]
+                sine = pltpu.roll(pltpu.roll(part, 64, 1), 124, 0)
+                pieces.append(jnp.where(upper, part * sign - sine, 0.0).astype(BF))
+        return dot(jnp.concatenate(pieces, axis=0), perm[...], TN)
 
     def to_owner(src, dst, i):
         def step(r, carry):
@@ -204,32 +181,24 @@
             lax.fori_loop(1, dps, step, 0)
         pltpu.make_async_copy(src.at[dpi], dst.at[dpi], dp_recv.at[i]).start()
 
-    def give_partner(i, b):
-        pltpu.make_async_remote_copy(
-            src_ref=ya.at[i, b, half],
-            dst_ref=ya.at[i, b, half],
-            send_sem=x_send.at[2 + i, b],
-            recv_sem=x_recv.at[2 + i, b],
-            device_id={"pencil": partner},
-            device_id_type=MESH,
-        ).start()
-
     def rows_back(i, b, phase):
-        x_wait(2 + i, b, ya.at[i, b, other])
-        turned = dot(perm[:, :256], ya[i, b, 0], NT) + dot(perm[:, 256:], ya[i, b, 1], NT)
-        turned = turned.astype(BF)
+        turned = dot(perm[...], ya[i, b], NT).astype(BF)
         lhs = jnp.concatenate([turned[c * 128 : (c + 1) * 128] for c in range(4)], axis=1)
-        for dy, dc in PEERS + ((0, 0),):
-            to = peer_of(dy, dc)
+        upper = lax.broadcasted_iota(jnp.int32, (128, 128), 0) % 8 < 4
+        for steps in PEERS + ((0, 0, 0),):
+            to = peer_of(*steps)
             lines = dot(lhs, inv[:, pl.ds(pl.multiple_of(to * 256, 256), 256)])
-            both = jnp.concatenate(
-                [lines[:, :128].reshape(16, 8, 128), lines[:, 128:].reshape(16, 8, 128)], axis=1
-            )
-            send[phase, b, to] = both.reshape(256, 128).astype(BF)
-            if (dy, dc) == (0, 0):
+            send[phase, b, to] = jnp.where(upper, lines[:, :128], lines[:, 128:]).astype(BF)
+            if steps == (0, 0, 0):
                 keep_own(b, phase)
             else:
                 send_one(b, phase, to)
+
+    def field(ref, n):
+        tile = ref[:, pl.ds(pl.multiple_of(n * 16, 16), 16), :].astype(F32)
+        for i in range(2):
+            lines = tile[:, i * 8 : (i + 1) * 8].reshape(128, 128).astype(BF)
+            yield pl.ds(pl.multiple_of(n * 8 + i * 4, 4), 4), dot(lines, col[...], TN)
 
     def mix_points(values, b, matrix, add, tiles=(0, 2)):
         def step(t, carry):
@@ -262,7 +231,7 @@
         return pl.ds(pl.multiple_of(pair % pairs * 16, 16), 16)
 
     def mix_modes(b):
-        spec = spectrum(0, b)
+        spec = spectrum(b, 0).astype(BF).astype(F32)
         for ri in range(2):
             for j in range(4):
                 for p in range(2):
@@ -297,12 +266,12 @@
             first, second = modes[2 * p], modes[2 * p + 1]
             real = jnp.where(low, first, pltpu.roll(second, 64, 1))
             imag = jnp.where(low, pltpu.roll(first, 64, 1), second)
-            ya[0, b, half, 0:64, p * 128 : (p + 1) * 128] = real.astype(BF)
-            ya[0, b, half, 64:128, p * 128 : (p + 1) * 128] = imag.astype(BF)
-        give_partner(0, b)
+            ya[0, b, 0:64, p * 128 : (p + 1) * 128] = real.astype(BF)
+            ya[0, b, 64:128, p * 128 : (p + 1) * 128] = imag.astype(BF)
+        rows_back(0, b, 1)
 
     def grad_modes(b):
-        spec = spectrum(1, b)
+        spec = spectrum(b, 2)
         for p in range(2):
             part = spec[:, p * 128 : (p + 1) * 128]
             part = part * (scale_lane if p == 0 else 2.0 / 262144.0)
@@ -332,21 +301,20 @@
             for ri in range(2):
                 first = dd[p, pl.ds(ri * 4 + 2 * p, 64, stride=8), :]
                 second = dd[p, pl.ds(ri * 4 + 2 * p + 1, 64, stride=8), :]
-                ya[1, b, half, ri * 64 : (ri + 1) * 64, p * 128 : (p + 1) * 128] = jnp.where(
+                ya[1, b, ri * 64 : (ri + 1) * 64, p * 128 : (p + 1) * 128] = jnp.where(
                     low, first, second
                 ).astype(BF)
-        give_partner(1, b)
+        rows_back(1, b, 3)
 
     def activation(b, chunks):
         def step(n, carry):
-            at = pl.ds(pl.multiple_of(n * 4, 4), 4)
-            lines = recv[1, b, :, pl.ds(pl.multiple_of(n * 16, 16), 16), :].reshape(128, 128)
-            z = dot(lines, col[...], TN) + zs[b, at].reshape(128, 512)
-            grad = cv[b, at].reshape(128, 512).astype(F32) * derivative(z)
-            dz[b, at] = grad.astype(BF).reshape(4, 32, 512)
-            return carry
-
-        lax.fori_loop(*chunks, step, 0, unroll=4)
+            for at, got in field(recv.at[1, b], n):
+                z = got + zs[b, at].reshape(128, 512)
+                grad = cv[b, at].reshape(128, 512).astype(F32) * derivative(z)
+                dz[b, at] = grad.astype(BF).reshape(4, 32, 512)
+            return carry
+
+        lax.fori_loop(*chunks, step, 0, unroll=2)
 
     def leave(b):
         pltpu.make_async_copy(xv.at[b], side.at[b], out_sem.at[b]).start()
@@ -355,13 +323,12 @@
         arrived(0, 3)
 
         def step(n, carry):
-            at = pl.ds(pl.multiple_of(n * 4, 4), 4)
-            lines = recv[3, 0, :, pl.ds(pl.multiple_of(n * 16, 16), 16), :].reshape(128, 128)
-            got = dot(lines, col[...], TN) + xv[0, at].reshape(128, 512).astype(F32)
-            xv[0, at] = got.astype(BF).reshape(4, 32, 512)
-            return carry
-
-        lax.fori_loop(0, 16, step, 0, unroll=4)
+            for at, got in field(recv.at[3, 0], n):
+                got = got + xv[0, at].reshape(128, 512).astype(F32)
+                xv[0, at] = got.astype(BF).reshape(4, 32, 512)
+            return carry
+
+        lax.fori_loop(0, 8, step, 0, unroll=2)
         leave(0)
 
     def weight_grad():
@@ -380,14 +347,14 @@
 
     col_wait()
     columns(xv, 0, 0)
-    pl.semaphore_wait(barrier, GROUP - 1 + 1 + dps - 1)
+    pl.semaphore_wait(barrier, GROUP - 1 + dps - 1)
     scatter(0, 0)
-    fwd_wait = load(fwd_h.at[half], fwd, 4, 1)
+    fwd_wait = load(fwd_h, fwd, 4, 1)
     perm_wait = load(perm_h, perm, 2, 2)
     columns(xv, 1, 0)
     scatter(1, 0)
     weight_wait = load(weight, wv, 16, 3)
-    inv_wait = load(inv_h.at[half], inv, 4, 4)
+    inv_wait = load(inv_h, inv, 8, 4)
     cot_waits = [load(cot.at[b], cv.at[b], 8, 5 + b) for b in range(2)]
 
     row = lax.broadcasted_iota(jnp.int32, (512, 64), 0)
@@ -407,33 +374,26 @@
 
     fwd_wait()
     perm_wait()
-    rows_forward(0, 0, 0)
-    mix_points(xv, 1, kf, bcol)
-    rows_forward(1, 0, 0)
+    inv_wait()
     weight_wait()
     mix_modes(0)
+    mix_points(xv, 1, kf, bcol)
     mix_modes(1)
-    inv_wait()
-    rows_back(0, 0, 1)
     to_owner(xb, xbr, 0)
-    rows_back(0, 1, 1)
 
     for b in range(2):
         arrived(b, 1)
         cot_waits[b]()
-        activation(b, (0, 16))
+        activation(b, (0, 8))
         columns(dz, b, 2)
         scatter(b, 2)
-    rows_forward(0, 2, 1)
-    mix_points(dz, 0, kb, None)
+    grad_modes(0)
+    mix_points(dz, 0, kb, None, (0, 1))
+    grad_modes(1)
+    to_owner(gb, gbr, 1)
+    mix_points(dz, 0, kb, None, (1, 2))
     mix_points(dz, 1, kb, None)
     leave(1)
-    rows_forward(1, 2, 1)
-    grad_modes(0)
-    grad_modes(1)
-    rows_back(1, 0, 3)
-    to_owner(gb, gbr, 1)
-    rows_back(1, 1, 3)
     finish_first()
     weight_grad()
 
@@ -441,8 +401,6 @@
         for b in range(2):
             sent = send.at[phase, b, pl.ds(0, GROUP - 1)]
             pltpu.make_async_copy(sent, sent, a2a_send.at[phase, b]).wait()
-            ref = xr.at[0, b]
-            pltpu.make_async_copy(ref, ref, x_send.at[phase, b]).wait()
     if dps > 1:
         for i, ref in enumerate((xb, gb)):
             sent = ref.at[pl.ds(0, dps - 1)]
@@ -473,10 +431,10 @@
 
     def step(n, carry):
         piece(1, n).wait()
+        tile = lv[:, pl.ds(pl.multiple_of(n * 16, 16), 16), :].astype(F32)
         for i in range(2):
             at = pl.ds(pl.multiple_of(n * 8 + i * 4, 4), 4)
-            rows = pl.ds(pl.multiple_of((2 * n + i) * 16, 16), 16)
-            part = lv[:, rows, :].reshape(128, 128)
+            part = tile[:, i * 8 : (i + 1) * 8].reshape(128, 128).astype(BF)
             got = dot(part, col[...], TN) + sv[1, at].reshape(128, 512).astype(F32)
             sv[1, at] = got.astype(BF).reshape(4, 32, 512)
         write(1, n)
@@ -504,7 +462,7 @@
         functools.partial(kernel, dps),
         out_shape=(
             jax.ShapeDtypeStruct((2, 64, 32, 512), BF),
-            jax.ShapeDtypeStruct((GROUP, 256, 128), BF),
+            jax.ShapeDtypeStruct((GROUP, 128, 128), BF),
             grad_shape,
         ),
         in_specs=[any_spec] * 3 + [vmem] * 2 + [any_spec] * 4,
@@ -514,16 +472,14 @@
             pltpu.VMEM((2, 64, 32, 512), BF),
             pltpu.VMEM((64, 4, 64, 128), BF),
             pltpu.VMEM((128, 512), BF),
-            pltpu.VMEM((1024, 512), BF),
-            pltpu.VMEM((512, 2048), BF),
-            pltpu.VMEM((512, 512), BF),
-            pltpu.VMEM((4, 2, GROUP, 256, 128), BF),
-            pltpu.VMEM((4, 2, GROUP, 256, 128), BF),
+            pltpu.VMEM((2048, 512), BF),
+            pltpu.VMEM((512, 4096), BF),
+            pltpu.VMEM((512, 256), BF),
+            pltpu.VMEM((4, 2, GROUP, 128, 128), BF),
+            pltpu.VMEM((4, 2, GROUP, 128, 128), BF),
             pltpu.VMEM((2, 64, 32, 512), F32),
             pltpu.VMEM((2, 64, 32, 512), BF),
-            pltpu.VMEM((2, 2, 2, 128, 256), BF),
             pltpu.VMEM((2, 2, 128, 256), BF),
-            pltpu.VMEM((2, 2, 2, 128, 256), BF),
             pltpu.VMEM((2, 512, 128), F32),
             pltpu.VMEM((dps, 2, per, 256), BF),
             pltpu.VMEM((dps, 2, per, 256), BF),
@@ -537,8 +493,6 @@
             pltpu.VMEM((512, 128), F32),
             dma((7,)),
             dma((2, 8)),
-            dma((4, 2)),
-            dma((4, 2)),
             dma((4, 2)),
             dma((4, 2)),
             dma((2,)),
@@ -559,7 +513,7 @@
         out_specs=(any_spec, any_spec),
         scratch_shapes=[
             pltpu.VMEM((2, 64, 32, 512), BF),
-            pltpu.VMEM((GROUP, 256, 128), BF),
+            pltpu.VMEM((GROUP, 128, 128), BF),
             pltpu.VMEM((128, 512), BF),
             pltpu.VMEM(grad_shape.shape, F32),
             dma((2, 8)),

time: 88.2 us -> 82.4 us (0.934); the launches traced: 88 us -> 81.2 us
  Pallas kernels: 87.4 us -> 80.4 us
    pallas_call x1, Pallas kernels: 82 us -> 75.1 us  [shards(): pl.pallas_call(functools.partial(kernel, dps), out_shape=(jax.ShapeDtypeS...]
where the time goes in v4:
time: 82.4 us; the launch traced here: 81.2 us
  Pallas kernels  80.4 us (98%)
    pallas_call x1, Pallas kernels, shards(): pl.pallas_call(functools.partial(kernel, dps), out_shape=(jax.ShapeDtypeS...  75.1 us
    pallas_call x1, Pallas kernels, shards(): pl.pallas_call(finish, out_shape=(jax.ShapeDtypeStruct((2, 64, 32, 512),...  5.35 us

profile of v4, /device:TPU:1, one launch (start us, length us, event | category | flops | bytes accessed | tf_op | source)
XLA Modules:
  0.0 81.2 jit_solution(17971683792152256486)
XLA Ops:
  0.6 75.1 %shard_map.104 = (bf16[2,64,32,512]{3,2,1,0:T(8,128)(2,1)}, bf16[16,128,128]{2,1,0:T(8,128)(2,1)}, f32[4,4,64,128]{3,2,1,0:T(8,128)}) custom-call(bf16[2,64,32,512]{3,2,1,0:T(8,128)(2,1)} %clips.1, bf16[2,64,32,512]{3,2,1,0:T(8,128)(2,1)} %cot.1, bf16[64,4,64,128]{3,2,1,0:T(8,128)(2,1)} %weight.1, bf16[64,64]{1,0:T(8,128)(2,1)} %pw.1, ...), custom_call_target="tpu_custom_call" | custom-call | flops 20000000000 | bytes 20000000 | tf_op jit(solution)/shard_map/pallas_call | solution.py:461
  75.7 5.3 %shard_map.105 = (bf16[2,64,32,512]{3,2,1,0:T(8,128)(2,1)}, f32[4,4,64,128]{3,2,1,0:T(8,128)}) custom-call(bf16[2,64,32,512]{3,2,1,0:T(8,128)(2,1)} %get-tuple-element.5.side, bf16[16,128,128]{2,1,0:T(8,128)(2,1)} %get-tuple-element.6.lines, bf16[128,512]{1,0:T(8,128)(2,1)} %constant.8.clone.col_h, f32[4,4,64,128]{3,2,1,0:T(8,128)} %get-tuple-element.7.sgrad), custom_call_target="tpu_custom_call" | custom-call | flops 600000000 | bytes 10000000 | tf_op jit(solution)/shard_map/pallas_call | solution.py:509

commit v5 on v4

--- a/solution.py
+++ b/solution.py
@@ -47,16 +47,15 @@
 
 
 def derivative(z):
-    a = jnp.abs(z)
-    e = jnp.exp(z * z * -0.5)
-    d = 1.0 + (0.3275911 / math.sqrt(2.0)) * a
-    t = pl.reciprocal(d, approx=True)
-    t = t * (2.0 - d * t)
-    poly = 1.061405429 * 0.5
+    e = jnp.exp2(z * z * (-0.5 / math.log(2.0))).astype(BF)
+    d = 1.0 + (0.3275911 / math.sqrt(2.0)) * jnp.abs(z)
+    t = pl.reciprocal(d, approx=True).astype(BF)
+    z = z.astype(BF)
+    poly = jnp.full_like(t, 1.061405429 * 0.5)
     for c in (-1.453152027, 1.421413741, -0.284496736, 0.254829592):
-        poly = poly * t + 0.5 * c
-    q = e * (poly * t - a * (1.0 / math.sqrt(TWO_PI)))
-    return jnp.where(z >= 0.0, 1.0 - q, q)
+        poly = poly * t + jnp.asarray(0.5 * c, BF)
+    q = e * (poly * t - jnp.abs(z) * jnp.asarray(1.0 / math.sqrt(TWO_PI), BF))
+    return jnp.where(z >= 0, 1 - q, q)
 
 
 PEERS = tuple((dx, dy, dc) for dx in (1, 0) for dy in (2, 1, 3, 0) for dc in (1, 0))[:-1]
@@ -114,15 +113,16 @@
     def slots(b, phase):
         return last if (phase, b) == (3, 1) else recv.at[phase, b]
 
-    def columns(values, b, phase):
+    def columns(rows, b, phase, n):
+        part = dot(col[...], rows, NT)
+        pieces = [part[:, i * 128 : (i + 1) * 128].reshape(GROUP, 8, 128) for i in range(2)]
+        at = pl.ds(pl.multiple_of(n * 16, 16), 16)
+        send[phase, b, :, at, :] = jnp.concatenate(pieces, axis=1).astype(BF)
+
+    def clip_columns(b):
         def step(n, carry):
-            if values is xv:
-                clip_piece(b, n).wait()
-            rows = values[b, pl.ds(pl.multiple_of(n * 8, 8), 8)].reshape(256, 512)
-            part = dot(col[...], rows, NT)
-            pieces = [part[:, i * 128 : (i + 1) * 128].reshape(GROUP, 8, 128) for i in range(2)]
-            at = pl.ds(pl.multiple_of(n * 16, 16), 16)
-            send[phase, b, :, at, :] = jnp.concatenate(pieces, axis=1).astype(BF)
+            clip_piece(b, n).wait()
+            columns(xv[b, pl.ds(pl.multiple_of(n * 8, 8), 8)].reshape(256, 512), b, 0, n)
             return carry
 
         lax.fori_loop(0, 8, step, 0, unroll=2)
@@ -308,10 +308,12 @@
 
     def activation(b, chunks):
         def step(n, carry):
+            grads = []
             for at, got in field(recv.at[1, b], n):
                 z = got + zs[b, at].reshape(128, 512)
-                grad = cv[b, at].reshape(128, 512).astype(F32) * derivative(z)
-                dz[b, at] = grad.astype(BF).reshape(4, 32, 512)
+                grads.append(cv[b, at].reshape(128, 512) * derivative(z))
+                dz[b, at] = grads[-1].reshape(4, 32, 512)
+            columns(jnp.concatenate(grads, axis=0), b, 2, n)
             return carry
 
         lax.fori_loop(*chunks, step, 0, unroll=2)
@@ -346,12 +348,12 @@
                 sgrad[2 * pair + i] = got[:, i * 128 : (i + 1) * 128].reshape(4, 64, 128)
 
     col_wait()
-    columns(xv, 0, 0)
+    clip_columns(0)
     pl.semaphore_wait(barrier, GROUP - 1 + dps - 1)
     scatter(0, 0)
     fwd_wait = load(fwd_h, fwd, 4, 1)
     perm_wait = load(perm_h, perm, 2, 2)
-    columns(xv, 1, 0)
+    clip_columns(1)
     scatter(1, 0)
     weight_wait = load(weight, wv, 16, 3)
     inv_wait = load(inv_h, inv, 8, 4)
@@ -385,7 +387,6 @@
         arrived(b, 1)
         cot_waits[b]()
         activation(b, (0, 8))
-        columns(dz, b, 2)
         scatter(b, 2)
     grad_modes(0)
     mix_points(dz, 0, kb, None, (0, 1))

time: 82.4 us -> 82.9 us (level)
  no operation moved by 1% of the time
where the time goes in v5:
time: 82.9 us; the launch traced here: 81.7 us
  Pallas kernels  80.9 us (98%)
    pallas_call x1, Pallas kernels, shards(): pl.pallas_call(functools.partial(kernel, dps), out_shape=(jax.ShapeDtypeS...  75.6 us
    pallas_call x1, Pallas kernels, shards(): pl.pallas_call(finish, out_shape=(jax.ShapeDtypeStruct((2, 64, 32, 512),...  5.33 us

profile of v5, /device:TPU:1, one launch (start us, length us, event | category | flops | bytes accessed | tf_op | source)
XLA Modules:
  0.0 81.7 jit_solution(2780047482469134158)
XLA Ops:
  0.6 75.6 %shard_map.104 = (bf16[2,64,32,512]{3,2,1,0:T(8,128)(2,1)}, bf16[16,128,128]{2,1,0:T(8,128)(2,1)}, f32[4,4,64,128]{3,2,1,0:T(8,128)}) custom-call(bf16[2,64,32,512]{3,2,1,0:T(8,128)(2,1)} %clips.1, bf16[2,64,32,512]{3,2,1,0:T(8,128)(2,1)} %cot.1, bf16[64,4,64,128]{3,2,1,0:T(8,128)(2,1)} %weight.1, bf16[64,64]{1,0:T(8,128)(2,1)} %pw.1, ...), custom_call_target="tpu_custom_call" | custom-call | flops 20000000000 | bytes 20000000 | tf_op jit(solution)/shard_map/pallas_call | solution.py:462
  76.2 5.3 %shard_map.105 = (bf16[2,64,32,512]{3,2,1,0:T(8,128)(2,1)}, f32[4,4,64,128]{3,2,1,0:T(8,128)}) custom-call(bf16[2,64,32,512]{3,2,1,0:T(8,128)(2,1)} %get-tuple-element.5.side, bf16[16,128,128]{2,1,0:T(8,128)(2,1)} %get-tuple-element.6.lines, bf16[128,512]{1,0:T(8,128)(2,1)} %constant.8.clone.col_h, f32[4,4,64,128]{3,2,1,0:T(8,128)} %get-tuple-element.7.sgrad), custom_call_target="tpu_custom_call" | custom-call | flops 600000000 | bytes 10000000 | tf_op jit(solution)/shard_map/pallas_call | solution.py:510

commit v6 on v5

--- a/solution.py
+++ b/solution.py
@@ -47,9 +47,9 @@
 
 
 def derivative(z):
-    e = jnp.exp2(z * z * (-0.5 / math.log(2.0))).astype(BF)
+    e = jnp.exp2((z * z * (-0.5 / math.log(2.0))).astype(BF))
     d = 1.0 + (0.3275911 / math.sqrt(2.0)) * jnp.abs(z)
-    t = pl.reciprocal(d, approx=True).astype(BF)
+    t = pl.reciprocal(d.astype(BF), approx=True).astype(BF)
     z = z.astype(BF)
     poly = jnp.full_like(t, 1.061405429 * 0.5)
     for c in (-1.453152027, 1.421413741, -0.284496736, 0.254829592):
@@ -68,7 +68,7 @@
     xv, cv, wv, col, fwd, inv, perm,
     send, recv, zs, dz, ya,
     xbf, xb, xbr, gbf, gb, gbr, dd, y3, kf, kb, bcol,
-    in_sem, clip_sem, a2a_send, a2a_recv, dp_send, dp_recv, out_sem,
+    in_sem, clip_sem, a2a_send, a2a_recv, dp_send, dp_recv,
 ):
     pen = lax.axis_index("pencil")
     dpi = lax.axis_index("dp")
@@ -216,7 +216,7 @@
                         zs[b, :, pl.ds(to, 8), lanes] = got.reshape(64, 8, 256)
                     parts.append(got.reshape(64, 8, 256))
                 if add is None:
-                    xv[b, :, pl.ds(at, 16), lanes] = jnp.concatenate(parts, axis=1).astype(BF)
+                    side[b, :, pl.ds(at, 16), lanes] = jnp.concatenate(parts, axis=1).astype(BF)
             return carry
 
         lax.fori_loop(*tiles, step, 0)
@@ -318,20 +318,16 @@
 
         lax.fori_loop(*chunks, step, 0, unroll=2)
 
-    def leave(b):
-        pltpu.make_async_copy(xv.at[b], side.at[b], out_sem.at[b]).start()
-
     def finish_first():
         arrived(0, 3)
 
         def step(n, carry):
             for at, got in field(recv.at[3, 0], n):
-                got = got + xv[0, at].reshape(128, 512).astype(F32)
-                xv[0, at] = got.astype(BF).reshape(4, 32, 512)
+                got = got + side[0, at].reshape(128, 512).astype(F32)
+                side[0, at] = got.astype(BF).reshape(4, 32, 512)
             return carry
 
         lax.fori_loop(0, 8, step, 0, unroll=2)
-        leave(0)
 
     def weight_grad():
         for i, ref in enumerate((xbr, gbr)):
@@ -394,7 +390,6 @@
     to_owner(gb, gbr, 1)
     mix_points(dz, 0, kb, None, (1, 2))
     mix_points(dz, 1, kb, None)
-    leave(1)
     finish_first()
     weight_grad()
 
@@ -406,49 +401,33 @@
         for i, ref in enumerate((xb, gb)):
             sent = ref.at[pl.ds(0, dps - 1)]
             pltpu.make_async_copy(sent, sent, dp_send.at[i]).wait()
-    for b in range(2):
-        pltpu.make_async_copy(xv.at[b], side.at[b], out_sem.at[b]).wait()
     arrived(1, 3)
 
 
-def finish(side, lines, col_h, sgrad, out, weights_out, sv, lv, col, gv, side_sem, sem):
-    def piece(b, n):
+def finish(side, lines, col_h, sgrad, out, weights_out, ov, col, sem):
+    col_copy = pltpu.make_async_copy(col_h, col, sem.at[0])
+    col_copy.start()
+    for n in range(8):
         at = pl.ds(n * 8, 8)
-        return pltpu.make_async_copy(side.at[b, at], sv.at[b, at], side_sem.at[b, n])
-
-    def write(b, n):
-        at = pl.ds(n * 8, 8)
-        pltpu.make_async_copy(sv.at[b, at], out.at[b, at], sem.at[3 + b]).start()
-
-    pltpu.make_async_copy(col_h, col, sem.at[0]).start()
-    for s in range(GROUP):
-        pltpu.make_async_copy(lines.at[s], lv.at[s], sem.at[1]).start()
-    for b in (1, 0):
-        for n in range(8):
-            piece(b, n).start()
-    pltpu.make_async_copy(sgrad, gv, sem.at[2]).start()
-    pltpu.make_async_copy(col, col, sem.at[0]).wait()
-    pltpu.make_async_copy(lv, lv, sem.at[1]).wait()
+        pltpu.make_async_copy(side.at[0, at], out.at[0, at], sem.at[1]).start()
+    away = pltpu.make_async_copy(sgrad, weights_out, sem.at[2])
+    away.start()
+    col_copy.wait()
 
     def step(n, carry):
-        piece(1, n).wait()
-        tile = lv[:, pl.ds(pl.multiple_of(n * 16, 16), 16), :].astype(F32)
+        tile = lines[:, pl.ds(pl.multiple_of(n * 16, 16), 16), :].astype(F32)
         for i in range(2):
             at = pl.ds(pl.multiple_of(n * 8 + i * 4, 4), 4)
             part = tile[:, i * 8 : (i + 1) * 8].reshape(128, 128).astype(BF)
-            got = dot(part, col[...], TN) + sv[1, at].reshape(128, 512).astype(F32)
-            sv[1, at] = got.astype(BF).reshape(4, 32, 512)
-        write(1, n)
-        piece(0, n).wait()
-        write(0, n)
+            got = dot(part, col[...], TN) + side[1, at].reshape(128, 512).astype(F32)
+            ov[at] = got.astype(BF).reshape(4, 32, 512)
+        at = pl.ds(n * 8, 8)
+        pltpu.make_async_copy(ov.at[at], out.at[1, at], sem.at[3]).start()
         return carry
 
     lax.fori_loop(0, 8, step, 0, unroll=2)
-    pltpu.make_async_copy(gv, gv, sem.at[2]).wait()
-    away = pltpu.make_async_copy(gv, weights_out, sem.at[5])
-    away.start()
-    for b in range(2):
-        pltpu.make_async_copy(sv.at[b], sv.at[b], sem.at[3 + b]).wait()
+    pltpu.make_async_copy(side.at[0], side.at[0], sem.at[1]).wait()
+    pltpu.make_async_copy(ov, ov, sem.at[3]).wait()
     away.wait()
 
 
@@ -462,12 +441,12 @@
     side, last, sgrad = pl.pallas_call(
         functools.partial(kernel, dps),
         out_shape=(
-            jax.ShapeDtypeStruct((2, 64, 32, 512), BF),
-            jax.ShapeDtypeStruct((GROUP, 128, 128), BF),
-            grad_shape,
+            pltpu.VMEM((2, 64, 32, 512), BF),
+            pltpu.VMEM((GROUP, 128, 128), BF),
+            pltpu.VMEM(grad_shape.shape, F32),
         ),
         in_specs=[any_spec] * 3 + [vmem] * 2 + [any_spec] * 4,
-        out_specs=(any_spec, any_spec, vmem),
+        out_specs=(vmem, vmem, vmem),
         scratch_shapes=[
             pltpu.VMEM((2, 64, 32, 512), BF),
             pltpu.VMEM((2, 64, 32, 512), BF),
@@ -498,10 +477,9 @@
             dma((4, 2)),
             dma((2,)),
             dma((2,)),
-            dma((2,)),
         ],
         compiler_params=pltpu.CompilerParams(
-            collective_id=0, has_side_effects=True, vmem_limit_bytes=60 * 1024 * 1024
+            collective_id=0, has_side_effects=True, vmem_limit_bytes=54 * 1024 * 1024
         ),
         cost_estimate=pl.CostEstimate(
             flops=20_000_000_000, bytes_accessed=20_000_000, transcendentals=4_000_000
@@ -510,17 +488,14 @@
     return pl.pallas_call(
         finish,
         out_shape=(jax.ShapeDtypeStruct((2, 64, 32, 512), BF), grad_shape),
-        in_specs=[any_spec] * 4,
+        in_specs=[vmem, vmem, any_spec, vmem],
         out_specs=(any_spec, any_spec),
         scratch_shapes=[
-            pltpu.VMEM((2, 64, 32, 512), BF),
-            pltpu.VMEM((GROUP, 128, 128), BF),
+            pltpu.VMEM((64, 32, 512), BF),
             pltpu.VMEM((128, 512), BF),
-            pltpu.VMEM(grad_shape.shape, F32),
-            dma((2, 8)),
-            dma((6,)),
+            dma((4,)),
         ],
-        compiler_params=pltpu.CompilerParams(vmem_limit_bytes=60 * 1024 * 1024),
+        compiler_params=pltpu.CompilerParams(vmem_limit_bytes=16 * 1024 * 1024),
         cost_estimate=pl.CostEstimate(
             flops=600_000_000, bytes_accessed=10_000_000, transcendentals=0
         ),

time: 82.9 us -> 78.9 us (0.952)
  the two profiles are of different devices: /device:TPU:1 before, /device:TPU:2 now
where the time goes in v6:
time: 78.9 us; the launch traced here: 78.8 us
  Pallas kernels  78 us (99%)
  between operations  0.82 us (1%)
    pallas_call x1, Pallas kernels, shards(): pl.pallas_call(functools.partial(kernel, dps), out_shape=(pltpu.VMEM((2,...  75.6 us
    pallas_call x1, Pallas kernels, shards(): pl.pallas_call(finish, out_shape=(jax.ShapeDtypeStruct((2, 64, 32, 512),...  2.36 us

profile of v6, /device:TPU:2, one launch (start us, length us, event | category | flops | bytes accessed | tf_op | source)
XLA Modules:
  0.0 78.8 jit_solution(2606157787567270944)
XLA Ops:
  0.6 0.0 copy-start
  0.6 75.6 %shard_map.104 = (bf16[2,64,32,512]{3,2,1,0:T(8,128)(2,1)S(1)}, bf16[16,128,128]{2,1,0:T(8,128)(2,1)S(1)}, f32[4,4,64,128]{3,2,1,0:T(8,128)S(1)}) custom-call(bf16[2,64,32,512]{3,2,1,0:T(8,128)(2,1)} %clips.1, bf16[2,64,32,512]{3,2,1,0:T(8,128)(2,1)} %cot.1, bf16[64,4,64,128]{3,2,1,0:T(8,128)(2,1)} %weight.1, bf16[64,64]{1,0:T(8,128)(2,1)} %pw.1, ...), custom_call_target="tpu_custom_call" | custom-call | flops 20000000000 | bytes 20000000 | tf_op jit(solution)/shard_map/pallas_call | solution.py:441
  76.3 0.0 copy-done
  76.3 2.4 %shard_map.105 = (bf16[2,64,32,512]{3,2,1,0:T(8,128)(2,1)}, f32[4,4,64,128]{3,2,1,0:T(8,128)}) custom-call(bf16[2,64,32,512]{3,2,1,0:T(8,128)(2,1)S(1)} %get-tuple-element.5.side, bf16[16,128,128]{2,1,0:T(8,128)(2,1)S(1)} %get-tuple-element.6.lines, bf16[128,512]{1,0:T(8,128)(2,1)S(1)} %copy-done, f32[4,4,64,128]{3,2,1,0:T(8,128)S(1)} %get-tuple-element.7.sgrad), custom_call_target="tpu_custom_call" | custom-call | flops 600000000 | bytes 10000000 | tf_op jit(solution)/shard_map/pallas_call | solution.py:488
Async XLA Ops:
  0.6 75.7 %copy-start = (bf16[128,512]{1,0:T(8,128)(2,1)S(1)}, bf16[128,512]{1,0:T(8,128)(2,1)}, u32[]{:S(2)}) copy-start(bf16[128,512]{1,0:T(8,128)(2,1)} %constant.8.clone.col_h) | copy-start | bytes 393220

commit v7 on v6

--- a/solution.py
+++ b/solution.py
@@ -58,7 +58,10 @@
     return jnp.where(z >= 0, 1 - q, q)
 
 
-PEERS = tuple((dx, dy, dc) for dx in (1, 0) for dy in (2, 1, 3, 0) for dc in (1, 0))[:-1]
+PEERS = (
+    (1, 2, 0), (0, 2, 1), (1, 1, 1), (0, 1, 0), (1, 3, 0), (0, 3, 1), (1, 0, 1), (0, 2, 0),
+    (1, 2, 1), (0, 1, 1), (1, 1, 0), (0, 3, 0), (1, 3, 1), (0, 0, 1), (1, 0, 0),
+)
 
 
 def kernel(

time: 78.9 us -> 77.8 us (0.986)
  the two profiles are of different devices: /device:TPU:2 before, /device:TPU:1 now
where the time goes in v7:
time: 77.8 us; the launch traced here: 76.8 us
  Pallas kernels  76 us (98%)
  between operations  0.82 us (1%)
    pallas_call x1, Pallas kernels, shards(): pl.pallas_call(functools.partial(kernel, dps), out_shape=(pltpu.VMEM((2,...  73.6 us
    pallas_call x1, Pallas kernels, shards(): pl.pallas_call(finish, out_shape=(jax.ShapeDtypeStruct((2, 64, 32, 512),...  2.36 us

profile of v7, /device:TPU:1, one launch (start us, length us, event | category | flops | bytes accessed | tf_op | source)
XLA Modules:
  0.0 76.8 jit_solution(5652758890843139278)
XLA Ops:
  0.6 0.0 copy-start
  0.6 73.6 %shard_map.104 = (bf16[2,64,32,512]{3,2,1,0:T(8,128)(2,1)S(1)}, bf16[16,128,128]{2,1,0:T(8,128)(2,1)S(1)}, f32[4,4,64,128]{3,2,1,0:T(8,128)S(1)}) custom-call(bf16[2,64,32,512]{3,2,1,0:T(8,128)(2,1)} %clips.1, bf16[2,64,32,512]{3,2,1,0:T(8,128)(2,1)} %cot.1, bf16[64,4,64,128]{3,2,1,0:T(8,128)(2,1)} %weight.1, bf16[64,64]{1,0:T(8,128)(2,1)} %pw.1, ...), custom_call_target="tpu_custom_call" | custom-call | flops 20000000000 | bytes 20000000 | tf_op jit(solution)/shard_map/pallas_call | solution.py:444
  74.3 0.0 copy-done
  74.3 2.4 %shard_map.105 = (bf16[2,64,32,512]{3,2,1,0:T(8,128)(2,1)}, f32[4,4,64,128]{3,2,1,0:T(8,128)}) custom-call(bf16[2,64,32,512]{3,2,1,0:T(8,128)(2,1)S(1)} %get-tuple-element.5.side, bf16[16,128,128]{2,1,0:T(8,128)(2,1)S(1)} %get-tuple-element.6.lines, bf16[128,512]{1,0:T(8,128)(2,1)S(1)} %copy-done, f32[4,4,64,128]{3,2,1,0:T(8,128)S(1)} %get-tuple-element.7.sgrad), custom_call_target="tpu_custom_call" | custom-call | flops 600000000 | bytes 10000000 | tf_op jit(solution)/shard_map/pallas_call | solution.py:491
Async XLA Ops:
  0.6 73.6 %copy-start = (bf16[128,512]{1,0:T(8,128)(2,1)S(1)}, bf16[128,512]{1,0:T(8,128)(2,1)}, u32[]{:S(2)}) copy-start(bf16[128,512]{1,0:T(8,128)(2,1)} %constant.8.clone.col_h) | copy-start | bytes 393220

commit v8 on v7

--- a/solution.py
+++ b/solution.py
@@ -130,10 +130,10 @@
 
         lax.fori_loop(0, 8, step, 0, unroll=2)
 
-    def send_one(b, phase, to):
+    def send_one(b, phase, to, rows=pl.ds(0, 128)):
         pltpu.make_async_remote_copy(
-            src_ref=send.at[phase, b, to],
-            dst_ref=slots(b, phase).at[pen],
+            src_ref=send.at[phase, b, to, rows],
+            dst_ref=slots(b, phase).at[pen, rows],
             send_sem=a2a_send.at[phase, b],
             recv_sem=a2a_recv.at[phase, b],
             device_id={"pencil": to},
@@ -378,15 +378,21 @@
     inv_wait()
     weight_wait()
     mix_modes(0)
+    mix_modes(1)
     mix_points(xv, 1, kf, bcol)
-    mix_modes(1)
+
+    cot_waits[0]()
+    arrived(0, 1)
+    activation(0, (0, 8))
+    scatter(0, 2)
     to_owner(xb, xbr, 0)
-
-    for b in range(2):
-        arrived(b, 1)
-        cot_waits[b]()
-        activation(b, (0, 8))
-        scatter(b, 2)
+    cot_waits[1]()
+    arrived(1, 1)
+    for n in range(2):
+        activation(1, (4 * n, 4 * n + 4))
+        for steps in PEERS:
+            send_one(1, 2, peer_of(*steps), pl.ds(n * 64, 64))
+    keep_own(1, 2)
     grad_modes(0)
     mix_points(dz, 0, kb, None, (0, 1))
     grad_modes(1)

time: 77.8 us -> 78.8 us (1.013); the launches traced: 76.8 us -> 78.7 us
  Pallas kernels: 76 us -> 77.9 us
    pallas_call x1, Pallas kernels: 73.6 us -> 75.5 us  [shards(): pl.pallas_call(functools.partial(kernel, dps), out_shape=(pltpu.VMEM((2,...]
where the time goes in v8:
time: 78.8 us; the launch traced here: 78.7 us
  Pallas kernels  77.9 us (99%)
  between operations  0.82 us (1%)
    pallas_call x1, Pallas kernels, shards(): pl.pallas_call(functools.partial(kernel, dps), out_shape=(pltpu.VMEM((2,...  75.5 us
    pallas_call x1, Pallas kernels, shards(): pl.pallas_call(finish, out_shape=(jax.ShapeDtypeStruct((2, 64, 32, 512),...  2.36 us

profile of v8, /device:TPU:1, one launch (start us, length us, event | category | flops | bytes accessed | tf_op | source)
XLA Modules:
  0.0 78.7 jit_solution(12956671136153655070)
XLA Ops:
  0.6 0.0 copy-start
  0.6 75.5 %shard_map.104 = (bf16[2,64,32,512]{3,2,1,0:T(8,128)(2,1)S(1)}, bf16[16,128,128]{2,1,0:T(8,128)(2,1)S(1)}, f32[4,4,64,128]{3,2,1,0:T(8,128)S(1)}) custom-call(bf16[2,64,32,512]{3,2,1,0:T(8,128)(2,1)} %clips.1, bf16[2,64,32,512]{3,2,1,0:T(8,128)(2,1)} %cot.1, bf16[64,4,64,128]{3,2,1,0:T(8,128)(2,1)} %weight.1, bf16[64,64]{1,0:T(8,128)(2,1)} %pw.1, ...), custom_call_target="tpu_custom_call" | custom-call | flops 20000000000 | bytes 20000000 | tf_op jit(solution)/shard_map/pallas_call | solution.py:450
  76.2 0.0 copy-done
  76.2 2.4 %shard_map.105 = (bf16[2,64,32,512]{3,2,1,0:T(8,128)(2,1)}, f32[4,4,64,128]{3,2,1,0:T(8,128)}) custom-call(bf16[2,64,32,512]{3,2,1,0:T(8,128)(2,1)S(1)} %get-tuple-element.5.side, bf16[16,128,128]{2,1,0:T(8,128)(2,1)S(1)} %get-tuple-element.6.lines, bf16[128,512]{1,0:T(8,128)(2,1)S(1)} %copy-done, f32[4,4,64,128]{3,2,1,0:T(8,128)S(1)} %get-tuple-element.7.sgrad), custom_call_target="tpu_custom_call" | custom-call | flops 600000000 | bytes 10000000 | tf_op jit(solution)/shard_map/pallas_call | solution.py:497
Async XLA Ops:
  0.6 75.5 %copy-start = (bf16[128,512]{1,0:T(8,128)(2,1)S(1)}, bf16[128,512]{1,0:T(8,128)(2,1)}, u32[]{:S(2)}) copy-start(bf16[128,512]{1,0:T(8,128)(2,1)} %constant.8.clone.col_h) | copy-start | bytes 393220

commit v9 on v8

--- a/solution.py
+++ b/solution.py
@@ -130,10 +130,10 @@
 
         lax.fori_loop(0, 8, step, 0, unroll=2)
 
-    def send_one(b, phase, to, rows=pl.ds(0, 128)):
+    def send_one(b, phase, to):
         pltpu.make_async_remote_copy(
-            src_ref=send.at[phase, b, to, rows],
-            dst_ref=slots(b, phase).at[pen, rows],
+            src_ref=send.at[phase, b, to],
+            dst_ref=slots(b, phase).at[pen],
             send_sem=a2a_send.at[phase, b],
             recv_sem=a2a_recv.at[phase, b],
             device_id={"pencil": to},
@@ -388,11 +388,8 @@
     to_owner(xb, xbr, 0)
     cot_waits[1]()
     arrived(1, 1)
-    for n in range(2):
-        activation(1, (4 * n, 4 * n + 4))
-        for steps in PEERS:
-            send_one(1, 2, peer_of(*steps), pl.ds(n * 64, 64))
-    keep_own(1, 2)
+    activation(1, (0, 8))
+    scatter(1, 2)
     grad_modes(0)
     mix_points(dz, 0, kb, None, (0, 1))
     grad_modes(1)

time: 78.8 us -> 78.4 us (level)
  no operation moved by 1% of the time
where the time goes in v9:
time: 78.4 us; the launch traced here: 78.2 us
  Pallas kernels  77.4 us (99%)
  between operations  0.82 us (1%)
    pallas_call x1, Pallas kernels, shards(): pl.pallas_call(functools.partial(kernel, dps), out_shape=(pltpu.VMEM((2,...  75.1 us
    pallas_call x1, Pallas kernels, shards(): pl.pallas_call(finish, out_shape=(jax.ShapeDtypeStruct((2, 64, 32, 512),...  2.36 us

profile of v9, /device:TPU:1, one launch (start us, length us, event | category | flops | bytes accessed | tf_op | source)
XLA Modules:
  0.0 78.2 jit_solution(16614115814991540389)
XLA Ops:
  0.6 0.0 copy-start
  0.6 75.1 %shard_map.104 = (bf16[2,64,32,512]{3,2,1,0:T(8,128)(2,1)S(1)}, bf16[16,128,128]{2,1,0:T(8,128)(2,1)S(1)}, f32[4,4,64,128]{3,2,1,0:T(8,128)S(1)}) custom-call(bf16[2,64,32,512]{3,2,1,0:T(8,128)(2,1)} %clips.1, bf16[2,64,32,512]{3,2,1,0:T(8,128)(2,1)} %cot.1, bf16[64,4,64,128]{3,2,1,0:T(8,128)(2,1)} %weight.1, bf16[64,64]{1,0:T(8,128)(2,1)} %pw.1, ...), custom_call_target="tpu_custom_call" | custom-call | flops 20000000000 | bytes 20000000 | tf_op jit(solution)/shard_map/pallas_call | solution.py:447
  75.7 0.0 copy-done
  75.7 2.4 %shard_map.105 = (bf16[2,64,32,512]{3,2,1,0:T(8,128)(2,1)}, f32[4,4,64,128]{3,2,1,0:T(8,128)}) custom-call(bf16[2,64,32,512]{3,2,1,0:T(8,128)(2,1)S(1)} %get-tuple-element.5.side, bf16[16,128,128]{2,1,0:T(8,128)(2,1)S(1)} %get-tuple-element.6.lines, bf16[128,512]{1,0:T(8,128)(2,1)S(1)} %copy-done, f32[4,4,64,128]{3,2,1,0:T(8,128)S(1)} %get-tuple-element.7.sgrad), custom_call_target="tpu_custom_call" | custom-call | flops 600000000 | bytes 10000000 | tf_op jit(solution)/shard_map/pallas_call | solution.py:494
Async XLA Ops:
  0.6 75.1 %copy-start = (bf16[128,512]{1,0:T(8,128)(2,1)S(1)}, bf16[128,512]{1,0:T(8,128)(2,1)}, u32[]{:S(2)}) copy-start(bf16[128,512]{1,0:T(8,128)(2,1)} %constant.8.clone.col_h) | copy-start | bytes 393220
